TPU v7x, 768 devices: a whole 4x8x12 slice. The times are simulated.
768 devices in a mesh: dp: 64 (over y, x, core), seq: 12 (over z).
Axes of the slice: x: 4, y: 8, z: 12, core: 2. Of those that a mesh axis runs over, the one named last changes fastest.
Arguments:
- queries: bfloat16 [12, 12288, 1024], P('seq', 'dp'), may hold values from -6 to 6
- keys: bfloat16 [12, 12288, 1024], P('seq', 'dp'), may hold values from -6 to 6
- values: bfloat16 [12, 12288, 1024], P('seq', 'dp'), may hold values from -6 to 6
- grad_out: bfloat16 [12, 12288, 1024], P('seq', 'dp'), may hold values from -6 to 6
- dest: int32 [12, 12288], P('seq', 'dp'), may hold values from 0 to 12287, as said below
- lengths: int32 [64, 4], P('dp'), may hold values from 1 to 768, 2304 in all within a row
Outputs:
- attended: bfloat16 [12, 12288, 1024], P('seq', 'dp')
- grad_queries: bfloat16 [12, 12288, 1024], P('seq', 'dp')
- grad_keys: bfloat16 [12, 12288, 1024], P('seq', 'dp')
- grad_values: bfloat16 [12, 12288, 1024], P('seq', 'dp')
Inputs may be any that keep to these rules, and one draw needn't show every extreme that they name: Each column of dest is a permutation of its 12288 balanced rows; balanced row r belongs to device r // 192; every loader device sends exactly 3 rows to every balanced device of its column. `lengths`: the histories of a pack fill its 2304 rows exactly; in every pack one history has 768 rows.
All inputs are finite; a program needn't handle non-finite values.
Results may differ from a plain program's by a relative error of at most 0.0055.
Values may be sent and summed in bfloat16 or wider, within the bound.
A program may use at most 64 MiB of HBM per device.

v0:
```python
import jax
import jax.numpy as jnp
from jax import lax
from jax.sharding import PartitionSpec as P

HEADS = 8
HDIM = 128


farthest = 4


def passed_along(block, axis, distance):
    devices = range(lax.axis_size(axis))
    route = [(i - distance, i) for i in devices if i - distance in devices]
    return lax.ppermute(block, axis, route)


def history_rows(block, row_count, history_ends, history_starts):
    global_rows = block * row_count + jnp.arange(row_count, dtype=jnp.int32)
    history_ids = jnp.sum((global_rows[:, None] >= history_ends[None, :]).astype(jnp.int32), axis=1)
    matched = history_ids[:, None] == jnp.arange(history_ends.shape[0], dtype=jnp.int32)[None, :]
    first_rows = jnp.sum(jnp.where(matched, history_starts[None, :], 0), axis=1)
    return (global_rows, history_ids, first_rows)


def pair_weight(query_rows, query_ids, key_rows, key_ids, row_scale):
    mask = (
        (query_ids[:, None] == key_ids[None, :])
        & (key_rows[None, :] <= query_rows[:, None])
        & (key_rows[None, :] >= 0)
    )
    return jnp.where(mask, row_scale[:, None], jnp.float32(0.0))


def block_terms(query, grad, key_part, value_part, weight):
    score_scale = HDIM ** (-0.5)
    scores = (
        jnp.einsum("qhd,khd->hqk", query, key_part, preferred_element_type=jnp.float32)
        * score_scale
    )
    gate_sig = jax.nn.sigmoid(scores)
    weight_heads = weight[None]
    mixing = (scores * gate_sig * weight_heads).astype(jnp.bfloat16)
    outputs = jnp.einsum("hqk,khd->qhd", mixing, value_part, preferred_element_type=jnp.float32)
    grad_mix = jnp.einsum("qhd,khd->hqk", grad, value_part, preferred_element_type=jnp.float32)
    grad_score = (grad_mix * weight_heads * gate_sig * (1.0 + scores * (1.0 - gate_sig))).astype(
        jnp.bfloat16
    )
    grad_query = (
        jnp.einsum("hqk,khd->qhd", grad_score, key_part, preferred_element_type=jnp.float32)
        * score_scale
    )
    grad_key = (
        jnp.einsum("hqk,qhd->khd", grad_score, query, preferred_element_type=jnp.float32)
        * score_scale
    )
    grad_value = jnp.einsum("hqk,qhd->khd", mixing, grad, preferred_element_type=jnp.float32)
    return (outputs, grad_query, grad_key, grad_value)


def shards(queries, keys, values, grad_out, dest, lengths):
    row_count = queries.shape[1]
    width = queries.shape[2]
    peer_count = lax.axis_size("dp")
    per_peer = row_count // peer_count
    targets = dest[0]
    send_order = jnp.argsort(targets)
    slot_out = (targets[send_order] % row_count).reshape(1, peer_count, per_peer)
    packet = jnp.stack([queries[0], keys[0], values[0], grad_out[0]])[:, send_order].reshape(
        4, peer_count, per_peer, width
    )
    packet_in, slot_in = (
        lax.all_to_all(packet, "dp", split_axis=1, concat_axis=1, tiled=True),
        lax.all_to_all(slot_out, "dp", split_axis=1, concat_axis=1, tiled=True),
    )
    slot_ids = slot_in.reshape(row_count)
    placed = packet_in.reshape(4, row_count, width)[:, jnp.argsort(slot_ids)]
    split_heads = placed.reshape(4, row_count, HEADS, HDIM)
    query = split_heads[0]
    key_own = split_heads[1]
    value_own = split_heads[2]
    grad = split_heads[3]
    block = lax.axis_index("seq")
    block_count = lax.axis_size("seq")
    reach = min(farthest, block_count - 1)
    longest = reach * row_count
    history_lengths = lengths[0]
    history_ends = jnp.cumsum(history_lengths)
    history_starts = history_ends - history_lengths
    query_rows, query_ids, query_first = history_rows(
        block, row_count, history_ends, history_starts
    )
    row_scale = jnp.full((row_count,), 1.0 / longest, jnp.float32)
    own_weight = pair_weight(query_rows, query_ids, query_rows, query_ids, row_scale)
    out_sum, grad_q_sum, grad_k_sum, grad_v_sum = block_terms(
        query, grad, key_own, value_own, own_weight
    )
    for distance in range(1, reach + 1):
        fetched_key, fetched_value = passed_along((key_own, value_own), "seq", distance)
        key_rows, key_ids, key_first = history_rows(
            block - distance, row_count, history_ends, history_starts
        )
        weight = pair_weight(query_rows, query_ids, key_rows, key_ids, row_scale)
        terms = block_terms(query, grad, fetched_key, fetched_value, weight)
        out_sum = out_sum + terms[0]
        grad_q_sum = grad_q_sum + terms[1]
        back_key, back_value = passed_along(
            (terms[2].astype(jnp.bfloat16), terms[3].astype(jnp.bfloat16)), "seq", -distance
        )
        grad_k_sum = grad_k_sum + back_key.astype(jnp.float32)
        grad_v_sum = grad_v_sum + back_value.astype(jnp.float32)
    results = jnp.stack(
        [
            out_sum.astype(jnp.bfloat16),
            grad_q_sum.astype(jnp.bfloat16),
            grad_k_sum.astype(jnp.bfloat16),
            grad_v_sum.astype(jnp.bfloat16),
        ]
    ).reshape(4, row_count, width)
    outgoing = results[:, slot_ids].reshape(4, peer_count, per_peer, width)
    returned = lax.all_to_all(outgoing, "dp", split_axis=1, concat_axis=1, tiled=True).reshape(
        4, row_count, width
    )
    restored = returned[:, jnp.argsort(send_order)]
    return (restored[0][None], restored[1][None], restored[2][None], restored[3][None])


def solution(mesh):
    return jax.shard_map(
        shards,
        mesh=mesh,
        in_specs=(
            P("seq", "dp", None),
            P("seq", "dp", None),
            P("seq", "dp", None),
            P("seq", "dp", None),
            P("seq", "dp"),
            P("dp", None),
        ),
        out_specs=(
            P("seq", "dp", None),
            P("seq", "dp", None),
            P("seq", "dp", None),
            P("seq", "dp", None),
        ),
        check_vma=False,
    )
```

profile of v0, /device:TPU:324, one launch (start us, length us, event | category | flops | bytes accessed | tf_op | source)
XLA Modules:
  0.0 494.6 jit_solution(11253060385666011937)
XLA Ops:
  0.7 3.9 sort.45
  7.4 10.6 %all-to-all-start.1 = ((s32[1,64,3]{2,0,1:T(1,128)}), s32[1,64,3]{2,0,1:T(1,128)S(1)}, u32[]{:S(2)}, u32[]{:S(2)}) async-start(s32[1,64,3]{2,0,1:T(1,128)} %bitcast.4), calls=%async_computation.1 | async-start | bytes 65536 | tf_op jit(solution)/shard_map/all_to_all | solution.py:75
  21.6 3.7 pad_maximum_fusion
  28.4 11.0 %all-to-all-start = ((bf16[4,64,3,1024]{3,0,2,1:T(4,128)(2,1)}), bf16[4,64,3,1024]{3,0,2,1:T(4,128)(2,1)S(1)}, u32[]{:S(2)}, u32[]{:S(2)}) async-start(bf16[4,64,3,1024]{3,0,2,1:T(4,128)(2,1)} %bitcast.2), calls=%async_computation | async-start | bytes 3145728 | tf_op jit(solution)/shard_map/all_to_all | solution.py:74
  45.7 33.7 %all-to-all-done = bf16[4,64,3,1024]{3,0,2,1:T(4,128)(2,1)S(1)} async-done(((bf16[4,64,3,1024]{3,0,2,1:T(4,128)(2,1)}), bf16[4,64,3,1024]{3,0,2,1:T(4,128)(2,1)S(1)}, u32[]{:S(2)}, u32[]{:S(2)}) %all-to-all-start) | async-done | bytes 1572896 | tf_op jit(solution)/shard_map/all_to_all | solution.py:74
  81.3 7.8 %slice_reduce_fusion.1 = (bf16[192,1024]{1,0:T(8,128)(2,1)S(1)}, bf16[192,1024]{1,0:T(8,128)(2,1)S(1)}, bf16[192,1024]{1,0:T(8,128)(2,1)S(1)}, bf16[192,1024]{1,0:T(8,128)(2,1)S(1)}) fusion(bf16[4,192,1024]{2,0,1:T(4,128)(2,1)S(1)} %bitcast.229), kind=kLoop, calls=%fused_computation.64 | loop fusion | bytes 3145728 | tf_op jit(solution)/shard_map/slice | solution.py:82
  89.2 6.7 %collective-permute-start.5 = (bf16[192,8,128]{2,0,1:T(8,128)(2,1)S(1)}, bf16[192,8,128]{2,0,1:T(8,128)(2,1)S(1)}, u32[]{:S(2)}, u32[]{:S(2)}) collective-permute-start(bf16[192,8,128]{2,0,1:T(8,128)(2,1)S(1)} %copy_bitcast_fusion.1), channel_id=1, source_target_pairs={{0,3},{1,4},{2,5},{3,6},{4,7},{5,8},{6,9},{7,10},{8,11},{12,15},{1... | collective-permute-start | bytes 1179656 | tf_op jit(solution)/shard_map/ppermute | solution.py:16
  95.9 4.3 collective-permute-start.3
  111.2 19.1 %collective-permute-start.2 = (bf16[192,8,128]{2,0,1:T(8,128)(2,1)S(1)}, bf16[192,8,128]{2,0,1:T(8,128)(2,1)S(1)}, u32[]{:S(2)}, u32[]{:S(2)}) collective-permute-start(bf16[192,8,128]{2,0,1:T(8,128)(2,1)S(1)} %copy_bitcast_fusion), channel_id=1, source_target_pairs={{0,2},{1,3},{2,4},{3,5},{4,6},{5,7},{6,8},{7,9},{8,10},{9,11},{12,... | collective-permute-start | bytes 1179656 | tf_op jit(solution)/shard_map/ppermute | solution.py:16
  131.0 79.9 %collective-permute-done.4 = bf16[192,8,128]{2,0,1:T(8,128)(2,1)S(1)} collective-permute-done((bf16[192,8,128]{2,0,1:T(8,128)(2,1)S(1)}, bf16[192,8,128]{2,0,1:T(8,128)(2,1)S(1)}, u32[]{:S(2)}, u32[]{:S(2)}) %collective-permute-start.4) | collective-permute-done | bytes 393248 | tf_op jit(solution)/shard_map/ppermute | solution.py:16
  215.4 26.2 %collective-permute-start = (bf16[192,8,128]{2,0,1:T(8,128)(2,1)S(1)}, bf16[192,8,128]{2,0,1:T(8,128)(2,1)S(1)}, u32[]{:S(2)}, u32[]{:S(2)}) collective-permute-start(bf16[192,8,128]{2,0,1:T(8,128)(2,1)S(1)} %copy_bitcast_fusion), channel_id=1, source_target_pairs={{0,1},{1,2},{2,3},{3,4},{4,5},{5,6},{6,7},{7,8},{8,9},{9,10},{10,1... | collective-permute-start | bytes 1179656 | tf_op jit(solution)/shard_map/ppermute | solution.py:16
  242.3 9.9 %collective-permute-start.10 = (bf16[192,8,128]{2,0,1:T(8,128)(2,1)S(1)}, bf16[192,8,128]{2,0,1:T(8,128)(2,1)S(1)}, u32[]{:S(2)}, u32[]{:S(2)}) collective-permute-start(bf16[192,8,128]{2,0,1:T(8,128)(2,1)S(1)} %fusion.14), channel_id=1, source_target_pairs={{3,0},{4,1},{5,2},{6,3},{7,4},{8,5},{9,6},{10,7},{11,8},{15,12},{1... | collective-permute-start | bytes 1179656 | tf_op jit(solution)/shard_map/ppermute | solution.py:16
  260.6 9.4 %collective-permute-start.9 = (bf16[192,8,128]{2,0,1:T(8,128)(2,1)S(1)}, bf16[192,8,128]{2,0,1:T(8,128)(2,1)S(1)}, u32[]{:S(2)}, u32[]{:S(2)}) collective-permute-start(bf16[192,8,128]{2,0,1:T(8,128)(2,1)S(1)} %fusion.15), channel_id=1, source_target_pairs={{2,0},{3,1},{4,2},{5,3},{6,4},{7,5},{8,6},{9,7},{10,8},{11,9},{14,... | collective-permute-start | bytes 1179656 | tf_op jit(solution)/shard_map/ppermute | solution.py:16
  275.2 6.5 %collective-permute-start.8 = (bf16[192,8,128]{2,0,1:T(8,128)(2,1)}, bf16[192,8,128]{2,0,1:T(8,128)(2,1)}, u32[]{:S(2)}, u32[]{:S(2)}) collective-permute-start(bf16[192,8,128]{2,0,1:T(8,128)(2,1)} %fusion.16), channel_id=1, source_target_pairs={{1,0},{2,1},{3,2},{4,3},{5,4},{6,5},{7,6},{8,7},{9,8},{10,9},{11,1... | collective-permute-start | bytes 1179656 | tf_op jit(solution)/shard_map/ppermute | solution.py:16
  286.8 13.6 %collective-permute-start.15 = (bf16[192,8,128]{2,0,1:T(8,128)(2,1)}, bf16[192,8,128]{2,0,1:T(8,128)(2,1)}, u32[]{:S(2)}, u32[]{:S(2)}) collective-permute-start(bf16[192,8,128]{2,0,1:T(8,128)(2,1)} %fusion.20), channel_id=1, source_target_pairs={{4,0},{5,1},{6,2},{7,3},{8,4},{9,5},{10,6},{11,7},{16,12},{17,13},... | collective-permute-start | bytes 1179656 | tf_op jit(solution)/shard_map/ppermute | solution.py:16
  300.5 49.6 %collective-permute-done.11 = bf16[192,8,128]{2,0,1:T(8,128)(2,1)S(1)} collective-permute-done((bf16[192,8,128]{2,0,1:T(8,128)(2,1)S(1)}, bf16[192,8,128]{2,0,1:T(8,128)(2,1)S(1)}, u32[]{:S(2)}, u32[]{:S(2)}) %collective-permute-start.11) | collective-permute-done | bytes 393248 | tf_op jit(solution)/shard_map/ppermute | solution.py:16
  352.0 4.7 collective-permute-done.9
  356.7 11.3 %collective-permute-start.12 = (bf16[192,8,128]{2,0,1:T(8,128)(2,1)}, bf16[192,8,128]{2,0,1:T(8,128)(2,1)}, u32[]{:S(2)}, u32[]{:S(2)}) collective-permute-start(bf16[192,8,128]{2,0,1:T(8,128)(2,1)} %fusion.17), channel_id=1, source_target_pairs={{1,0},{2,1},{3,2},{4,3},{5,4},{6,5},{7,6},{8,7},{9,8},{10,9},{11,1... | collective-permute-start | bytes 1179656 | tf_op jit(solution)/shard_map/ppermute | solution.py:16
  377.4 14.9 %collective-permute-done.15 = bf16[192,8,128]{2,0,1:T(8,128)(2,1)} collective-permute-done((bf16[192,8,128]{2,0,1:T(8,128)(2,1)}, bf16[192,8,128]{2,0,1:T(8,128)(2,1)}, u32[]{:S(2)}, u32[]{:S(2)}) %collective-permute-start.15) | collective-permute-done | bytes 393248 | tf_op jit(solution)/shard_map/ppermute | solution.py:16
  392.3 29.8 %collective-permute-done.13 = bf16[192,8,128]{2,0,1:T(8,128)(2,1)} collective-permute-done((bf16[192,8,128]{2,0,1:T(8,128)(2,1)}, bf16[192,8,128]{2,0,1:T(8,128)(2,1)}, u32[]{:S(2)}, u32[]{:S(2)}) %collective-permute-start.13) | collective-permute-done | bytes 393248 | tf_op jit(solution)/shard_map/ppermute | solution.py:16
  422.1 5.4 %collective-permute-done.12 = bf16[192,8,128]{2,0,1:T(8,128)(2,1)} collective-permute-done((bf16[192,8,128]{2,0,1:T(8,128)(2,1)}, bf16[192,8,128]{2,0,1:T(8,128)(2,1)}, u32[]{:S(2)}, u32[]{:S(2)}) %collective-permute-start.12) | collective-permute-done | bytes 393248 | tf_op jit(solution)/shard_map/ppermute | solution.py:16
  431.2 4.8 pad_maximum_fusion.1
  439.2 7.4 %all-to-all-start.2 = ((bf16[4,64,3,1024]{3,0,2,1:T(4,128)(2,1)}), bf16[4,64,3,1024]{3,0,2,1:T(4,128)(2,1)S(1)}, u32[]{:S(2)}, u32[]{:S(2)}) async-start(bf16[4,64,3,1024]{3,0,2,1:T(4,128)(2,1)} %bitcast.22), calls=%async_computation.2 | async-start | bytes 3145728 | tf_op jit(solution)/shard_map/all_to_all | solution.py:122
  449.8 36.9 %all-to-all-done.2 = bf16[4,64,3,1024]{3,0,2,1:T(4,128)(2,1)S(1)} async-done(((bf16[4,64,3,1024]{3,0,2,1:T(4,128)(2,1)}), bf16[4,64,3,1024]{3,0,2,1:T(4,128)(2,1)S(1)}, u32[]{:S(2)}, u32[]{:S(2)}) %all-to-all-start.2) | async-done | bytes 1572896 | tf_op jit(solution)/shard_map/all_to_all | solution.py:122
  (123 shorter events, 81.8 us)
Async XLA Ops:
  0.6 19.1 %copy-start.4 = (bf16[1,192,1024]{2,1,0:T(8,128)(2,1)S(1)}, bf16[1,192,1024]{2,1,0:T(8,128)(2,1)}, u32[]{:S(2)}) copy-start(bf16[1,192,1024]{2,1,0:T(8,128)(2,1)} %param.7) | copy-start | bytes 1179652
  7.4 21.1 %all-to-all-start.1 = ((s32[1,64,3]{2,0,1:T(1,128)}), s32[1,64,3]{2,0,1:T(1,128)S(1)}, u32[]{:S(2)}, u32[]{:S(2)}) async-start(s32[1,64,3]{2,0,1:T(1,128)} %bitcast.4), calls=%async_computation.1 | async-start | bytes 65536 | tf_op jit(solution)/shard_map/all_to_all | solution.py:75
  28.4 50.9 %all-to-all-start = ((bf16[4,64,3,1024]{3,0,2,1:T(4,128)(2,1)}), bf16[4,64,3,1024]{3,0,2,1:T(4,128)(2,1)S(1)}, u32[]{:S(2)}, u32[]{:S(2)}) async-start(bf16[4,64,3,1024]{3,0,2,1:T(4,128)(2,1)} %bitcast.2), calls=%async_computation | async-start | bytes 3145728 | tf_op jit(solution)/shard_map/all_to_all | solution.py:74
  89.1 18.4 %copy-start.9 = (f32[192,192]{1,0:T(8,128)S(1)}, f32[192,192]{1,0:T(8,128)}, u32[]{:S(2)}) copy-start(f32[192,192]{1,0:T(8,128)} %get-tuple-element.35) | copy-start | bytes 442372
  89.2 22.0 %collective-permute-start.5 = (bf16[192,8,128]{2,0,1:T(8,128)(2,1)S(1)}, bf16[192,8,128]{2,0,1:T(8,128)(2,1)S(1)}, u32[]{:S(2)}, u32[]{:S(2)}) collective-permute-start(bf16[192,8,128]{2,0,1:T(8,128)(2,1)S(1)} %copy_bitcast_fusion.1), channel_id=1, source_target_pairs={{0,3},{1,4},{2,5},{3,6},{4,7},{5,8},{6,9},{7,10},{8,11},{12,15},{1... | collective-permute-start | bytes 1179656 | tf_op jit(solution)/shard_map/ppermute | solution.py:16
  95.9 158.8 %collective-permute-start.3 = (bf16[192,8,128]{2,0,1:T(8,128)(2,1)S(1)}, bf16[192,8,128]{2,0,1:T(8,128)(2,1)S(1)}, u32[]{:S(2)}, u32[]{:S(2)}) collective-permute-start(bf16[192,8,128]{2,0,1:T(8,128)(2,1)S(1)} %copy_bitcast_fusion.1), channel_id=1, source_target_pairs={{0,2},{1,3},{2,4},{3,5},{4,6},{5,7},{6,8},{7,9},{8,10},{9,11},{12,... | collective-permute-start | bytes 1179656 | tf_op jit(solution)/shard_map/ppermute | solution.py:16
  100.2 160.3 %collective-permute-start.1 = (bf16[192,8,128]{2,0,1:T(8,128)(2,1)S(1)}, bf16[192,8,128]{2,0,1:T(8,128)(2,1)S(1)}, u32[]{:S(2)}, u32[]{:S(2)}) collective-permute-start(bf16[192,8,128]{2,0,1:T(8,128)(2,1)S(1)} %copy_bitcast_fusion.1), channel_id=1, source_target_pairs={{0,1},{1,2},{2,3},{3,4},{4,5},{5,6},{6,7},{7,8},{8,9},{9,10},{10,1... | collective-permute-start | bytes 1179656 | tf_op jit(solution)/shard_map/ppermute | solution.py:16
  103.6 111.7 %collective-permute-start.7 = (bf16[192,8,128]{2,0,1:T(8,128)(2,1)S(1)}, bf16[192,8,128]{2,0,1:T(8,128)(2,1)S(1)}, u32[]{:S(2)}, u32[]{:S(2)}) collective-permute-start(bf16[192,8,128]{2,0,1:T(8,128)(2,1)S(1)} %copy_bitcast_fusion.1), channel_id=1, source_target_pairs={{0,4},{1,5},{2,6},{3,7},{4,8},{5,9},{6,10},{7,11},{12,16},{13,17},... | collective-permute-start | bytes 1179656 | tf_op jit(solution)/shard_map/ppermute | solution.py:16
  105.6 105.3 %collective-permute-start.4 = (bf16[192,8,128]{2,0,1:T(8,128)(2,1)S(1)}, bf16[192,8,128]{2,0,1:T(8,128)(2,1)S(1)}, u32[]{:S(2)}, u32[]{:S(2)}) collective-permute-start(bf16[192,8,128]{2,0,1:T(8,128)(2,1)S(1)} %copy_bitcast_fusion), channel_id=1, source_target_pairs={{0,3},{1,4},{2,5},{3,6},{4,7},{5,8},{6,9},{7,10},{8,11},{12,15},{1... | collective-permute-start | bytes 1179656 | tf_op jit(solution)/shard_map/ppermute | solution.py:16
  109.1 21.1 %copy-start.8 = (f32[192,192]{1,0:T(8,128)S(1)}, f32[192,192]{1,0:T(8,128)}, u32[]{:S(2)}) copy-start(f32[192,192]{1,0:T(8,128)} %get-tuple-element.36) | copy-start | bytes 442372
  111.2 146.2 %collective-permute-start.2 = (bf16[192,8,128]{2,0,1:T(8,128)(2,1)S(1)}, bf16[192,8,128]{2,0,1:T(8,128)(2,1)S(1)}, u32[]{:S(2)}, u32[]{:S(2)}) collective-permute-start(bf16[192,8,128]{2,0,1:T(8,128)(2,1)S(1)} %copy_bitcast_fusion), channel_id=1, source_target_pairs={{0,2},{1,3},{2,4},{3,5},{4,6},{5,7},{6,8},{7,9},{8,10},{9,11},{12,... | collective-permute-start | bytes 1179656 | tf_op jit(solution)/shard_map/ppermute | solution.py:16
  210.9 31.4 %collective-permute-start.6 = (bf16[192,8,128]{2,0,1:T(8,128)(2,1)S(1)}, bf16[192,8,128]{2,0,1:T(8,128)(2,1)S(1)}, u32[]{:S(2)}, u32[]{:S(2)}) collective-permute-start(bf16[192,8,128]{2,0,1:T(8,128)(2,1)S(1)} %copy_bitcast_fusion), channel_id=1, source_target_pairs={{0,4},{1,5},{2,6},{3,7},{4,8},{5,9},{6,10},{7,11},{12,16},{13,17},... | collective-permute-start | bytes 1179656 | tf_op jit(solution)/shard_map/ppermute | solution.py:16
  213.6 28.0 %copy-start.7 = (f32[192,192]{1,0:T(8,128)S(1)}, f32[192,192]{1,0:T(8,128)}, u32[]{:S(2)}) copy-start(f32[192,192]{1,0:T(8,128)} %get-tuple-element.37) | copy-start | bytes 442372
  215.4 57.8 %collective-permute-start = (bf16[192,8,128]{2,0,1:T(8,128)(2,1)S(1)}, bf16[192,8,128]{2,0,1:T(8,128)(2,1)S(1)}, u32[]{:S(2)}, u32[]{:S(2)}) collective-permute-start(bf16[192,8,128]{2,0,1:T(8,128)(2,1)S(1)} %copy_bitcast_fusion), channel_id=1, source_target_pairs={{0,1},{1,2},{2,3},{3,4},{4,5},{5,6},{6,7},{7,8},{8,9},{9,10},{10,1... | collective-permute-start | bytes 1179656 | tf_op jit(solution)/shard_map/ppermute | solution.py:16
  242.3 44.5 %collective-permute-start.10 = (bf16[192,8,128]{2,0,1:T(8,128)(2,1)S(1)}, bf16[192,8,128]{2,0,1:T(8,128)(2,1)S(1)}, u32[]{:S(2)}, u32[]{:S(2)}) collective-permute-start(bf16[192,8,128]{2,0,1:T(8,128)(2,1)S(1)} %fusion.14), channel_id=1, source_target_pairs={{3,0},{4,1},{5,2},{6,3},{7,4},{8,5},{9,6},{10,7},{11,8},{15,12},{1... | collective-permute-start | bytes 1179656 | tf_op jit(solution)/shard_map/ppermute | solution.py:16
  254.8 122.7 %collective-permute-start.14 = (bf16[192,8,128]{2,0,1:T(8,128)(2,1)}, bf16[192,8,128]{2,0,1:T(8,128)(2,1)}, u32[]{:S(2)}, u32[]{:S(2)}) collective-permute-start(bf16[192,8,128]{2,0,1:T(8,128)(2,1)} %fusion.19), channel_id=1, source_target_pairs={{3,0},{4,1},{5,2},{6,3},{7,4},{8,5},{9,6},{10,7},{11,8},{15,12},{1... | collective-permute-start | bytes 1179656 | tf_op jit(solution)/shard_map/ppermute | solution.py:16
  257.4 92.6 %collective-permute-start.11 = (bf16[192,8,128]{2,0,1:T(8,128)(2,1)S(1)}, bf16[192,8,128]{2,0,1:T(8,128)(2,1)S(1)}, u32[]{:S(2)}, u32[]{:S(2)}) collective-permute-start(bf16[192,8,128]{2,0,1:T(8,128)(2,1)S(1)} %fusion.13), channel_id=1, source_target_pairs={{4,0},{5,1},{6,2},{7,3},{8,4},{9,5},{10,6},{11,7},{16,12},{17,13},... | collective-permute-start | bytes 1179656 | tf_op jit(solution)/shard_map/ppermute | solution.py:16
  260.6 96.1 %collective-permute-start.9 = (bf16[192,8,128]{2,0,1:T(8,128)(2,1)S(1)}, bf16[192,8,128]{2,0,1:T(8,128)(2,1)S(1)}, u32[]{:S(2)}, u32[]{:S(2)}) collective-permute-start(bf16[192,8,128]{2,0,1:T(8,128)(2,1)S(1)} %fusion.15), channel_id=1, source_target_pairs={{2,0},{3,1},{4,2},{5,3},{6,4},{7,5},{8,6},{9,7},{10,8},{11,9},{14,... | collective-permute-start | bytes 1179656 | tf_op jit(solution)/shard_map/ppermute | solution.py:16
  275.2 98.5 %collective-permute-start.8 = (bf16[192,8,128]{2,0,1:T(8,128)(2,1)}, bf16[192,8,128]{2,0,1:T(8,128)(2,1)}, u32[]{:S(2)}, u32[]{:S(2)}) collective-permute-start(bf16[192,8,128]{2,0,1:T(8,128)(2,1)} %fusion.16), channel_id=1, source_target_pairs={{1,0},{2,1},{3,2},{4,3},{5,4},{6,5},{7,6},{8,7},{9,8},{10,9},{11,1... | collective-permute-start | bytes 1179656 | tf_op jit(solution)/shard_map/ppermute | solution.py:16
  286.8 81.6 %copy-start.1 = (bf16[192,8,128]{2,0,1:T(8,128)(2,1)}, bf16[192,8,128]{2,0,1:T(8,128)(2,1)S(1)}, u32[]{:S(2)}) copy-start(bf16[192,8,128]{2,0,1:T(8,128)(2,1)S(1)} %collective-permute-done.10) | copy-start | bytes 1179652
  286.8 105.5 %collective-permute-start.15 = (bf16[192,8,128]{2,0,1:T(8,128)(2,1)}, bf16[192,8,128]{2,0,1:T(8,128)(2,1)}, u32[]{:S(2)}, u32[]{:S(2)}) collective-permute-start(bf16[192,8,128]{2,0,1:T(8,128)(2,1)} %fusion.20), channel_id=1, source_target_pairs={{4,0},{5,1},{6,2},{7,3},{8,4},{9,5},{10,6},{11,7},{16,12},{17,13},... | collective-permute-start | bytes 1179656 | tf_op jit(solution)/shard_map/ppermute | solution.py:16
  350.1 72.0 %collective-permute-start.13 = (bf16[192,8,128]{2,0,1:T(8,128)(2,1)}, bf16[192,8,128]{2,0,1:T(8,128)(2,1)}, u32[]{:S(2)}, u32[]{:S(2)}) collective-permute-start(bf16[192,8,128]{2,0,1:T(8,128)(2,1)} %fusion.18), channel_id=1, source_target_pairs={{2,0},{3,1},{4,2},{5,3},{6,4},{7,5},{8,6},{9,7},{10,8},{11,9},{14,... | collective-permute-start | bytes 1179656 | tf_op jit(solution)/shard_map/ppermute | solution.py:16
  356.7 70.8 %collective-permute-start.12 = (bf16[192,8,128]{2,0,1:T(8,128)(2,1)}, bf16[192,8,128]{2,0,1:T(8,128)(2,1)}, u32[]{:S(2)}, u32[]{:S(2)}) collective-permute-start(bf16[192,8,128]{2,0,1:T(8,128)(2,1)} %fusion.17), channel_id=1, source_target_pairs={{1,0},{2,1},{3,2},{4,3},{5,4},{6,5},{7,6},{8,7},{9,8},{10,9},{11,1... | collective-permute-start | bytes 1179656 | tf_op jit(solution)/shard_map/ppermute | solution.py:16
  439.2 47.5 %all-to-all-start.2 = ((bf16[4,64,3,1024]{3,0,2,1:T(4,128)(2,1)}), bf16[4,64,3,1024]{3,0,2,1:T(4,128)(2,1)S(1)}, u32[]{:S(2)}, u32[]{:S(2)}) async-start(bf16[4,64,3,1024]{3,0,2,1:T(4,128)(2,1)} %bitcast.22), calls=%async_computation.2 | async-start | bytes 3145728 | tf_op jit(solution)/shard_map/all_to_all | solution.py:122
  (6 other events, 61.7 us)
where the time goes:
time: 502 us; the launch traced here: 495 us
  waiting for transfers between devices  259 us (52%)
  starting transfers between devices  151 us (30%)
  local copies, waits for them, and re-layouts  39.2 us (8%)
  matrix products  22.4 us (4%)
  other arithmetic  21.6 us (4%)
    ppermute x16, waiting for transfers between devices, passed_along(): return lax.ppermute(block, axis, route)  188 us
    ppermute x16, starting transfers between devices, passed_along(): return lax.ppermute(block, axis, route)  122 us
    all_to_all x1, waiting for transfers between devices, shards(): lax.all_to_all(outgoing, 'dp', split_axis=1, concat_axis=1, tiled=True)  36.9 us
    all_to_all x1, waiting for transfers between devices, shards(): lax.all_to_all(packet, 'dp', split_axis=1, concat_axis=1, tiled=True)  33.7 us
    all_to_all x1, starting transfers between devices, shards(): lax.all_to_all(packet, 'dp', split_axis=1, concat_axis=1, tiled=True)  11 us
    all_to_all x1, starting transfers between devices, shards(): lax.all_to_all(slot_out, 'dp', split_axis=1, concat_axis=1, tiled=True)  10.6 us
  transfers between devices with their start and end apart: 19, of which 10 were waited for; matrix products, arithmetic and copies ran while one was open for 10% of the time, Pallas kernels for 0%

commit v1 on v0

v1 whole, which is shorter than its diff:
```python
import functools

import jax
import jax.numpy as jnp
from jax import lax
from jax.experimental import pallas as pl
from jax.experimental.pallas import tpu as pltpu
from jax.sharding import PartitionSpec as P

HDIM = 128
REACH = 4
MESH = pl.DeviceIdType.MESH


def dot_nt(a, b):
    return lax.dot_general(a, b, (((1,), (1,)), ((), ())), preferred_element_type=jnp.float32)


def dot_tn(a, b):
    return lax.dot_general(a, b, (((0,), (0,)), ((), ())), preferred_element_type=jnp.float32)


def dot_nn(a, b):
    return lax.dot_general(a, b, (((1,), (0,)), ((), ())), preferred_element_type=jnp.float32)


def pair_weight(lengths_ref, query_first, query_count, key_first, key_count):
    shape = (query_count, key_count)
    query_rows = query_first + lax.broadcasted_iota(jnp.int32, shape, 0)
    key_rows = key_first + lax.broadcasted_iota(jnp.int32, shape, 1)
    start = jnp.int32(0)
    first_rows = jnp.zeros(shape, jnp.int32)
    for c in range(lengths_ref.shape[1]):
        start = start + lengths_ref[0, c]
        first_rows = jnp.where(query_rows >= start, start, first_rows)
    mask = (key_rows >= first_rows) & (key_rows <= query_rows)
    return mask


def pair_terms(query, grad, key, value, weight):
    scale = HDIM ** (-0.5)
    scores = dot_nt(query, key) * scale
    sig = 0.5 + 0.5 * jnp.tanh(0.5 * scores)
    mixing = (scores * sig * weight).astype(jnp.bfloat16)
    grad_mix = dot_nt(grad, value)
    grad_score = (grad_mix * weight * sig * (1.0 + scores * (1.0 - sig))).astype(jnp.bfloat16)
    outputs = dot_nn(mixing, value)
    grad_query = dot_nn(grad_score, key) * scale
    grad_key = dot_tn(grad_score, query) * scale
    grad_value = dot_tn(mixing, grad)
    return outputs, grad_query, grad_key, grad_value


def attend_kernel(
    axis,
    lengths_ref,
    slots_ref,
    loaded_ref,
    out_ref,
    keys,
    queries,
    far_out,
    far_in,
    near_out,
    near_in,
    near_sum,
    own_sum,
    weight_own,
    weight_near,
    weight_far,
    in_sems,
    out_sems,
):
    heads = keys.shape[0]
    rows = loaded_ref.shape[1]
    count = lax.axis_size(axis)
    block = lax.axis_index(axis)
    right = {axis: lax.rem(block + 1, count)}
    left = {axis: lax.rem(block + count - 1, count)}

    barrier = pltpu.get_barrier_semaphore()
    for neighbour in (left, right):
        pl.semaphore_signal(barrier, inc=1, device_id=neighbour, device_id_type=MESH)
    pl.semaphore_wait(barrier, 2)

    def copy(src, dst, sems, which, h, target):
        return pltpu.make_async_remote_copy(
            src_ref=src,
            dst_ref=dst,
            send_sem=sems.at[0, which, h],
            recv_sem=sems.at[1, which, h],
            device_id=target,
            device_id_type=MESH,
        )

    def near_copies(h):
        return (
            copy(keys.at[h, :, pl.ds(2 * rows, rows)], keys.at[h, :, pl.ds(rows, rows)], in_sems, 0, h, right),
            copy(queries.at[h, :, pl.ds(0, rows)], queries.at[h, :, pl.ds(rows, rows)], in_sems, 1, h, left),
        )

    def far_copies(h):
        return (
            copy(keys.at[h, :, pl.ds(rows, rows)], keys.at[h, :, pl.ds(0, rows)], in_sems, 2, h, right),
            copy(queries.at[h, :, pl.ds(rows, rows)], queries.at[h, :, pl.ds(2 * rows, rows)], in_sems, 3, h, left),
        )

    def far_returns(h):
        return (
            copy(far_out.at[h, 0], far_in.at[h, 0], out_sems, 0, h, right),
            copy(far_out.at[h, 1], far_in.at[h, 1], out_sems, 1, h, left),
        )

    def near_returns(h):
        return (
            copy(near_out.at[h, 0], near_in.at[h, 0], out_sems, 2, h, right),
            copy(near_out.at[h, 1], near_in.at[h, 1], out_sems, 3, h, left),
        )

    slots = slots_ref[0:1, :]
    place = jnp.where(
        lax.broadcasted_iota(jnp.int32, (rows, rows), 0) == slots, jnp.float32(1.0), jnp.float32(0.0)
    )
    unplace = place.T.astype(jnp.bfloat16)
    place = place.astype(jnp.bfloat16)
    for pair in range(heads // 2):
        lanes = pl.ds(pair * 2 * HDIM, 2 * HDIM)
        for a, (buffer, k, start) in enumerate(
            ((queries, 0, 0), (keys, 0, 2 * rows), (keys, 1, 2 * rows), (queries, 1, 0))
        ):
            placed = dot_nn(place, loaded_ref[a, :, lanes]).astype(jnp.bfloat16)
            buffer[2 * pair, k, pl.ds(start, rows), :] = placed[:, :HDIM]
            buffer[2 * pair + 1, k, pl.ds(start, rows), :] = placed[:, HDIM:]
        for h in (2 * pair, 2 * pair + 1):
            for c in near_copies(h):
                c.start()

    weight = jnp.float32(1.0 / (REACH * rows))
    first = block * rows
    for ref, query_first, key_first in (
        (weight_own, first, first - rows),
        (weight_near, first + rows, first - 2 * rows),
        (weight_far, first + 2 * rows, first - 2 * rows),
    ):
        mask = pair_weight(lengths_ref, query_first, ref.shape[0], key_first, ref.shape[1])
        ref[...] = jnp.where(mask, weight, jnp.float32(0.0))

    def forward(h, carry):
        for c in near_copies(h):
            c.wait_recv()
        for c in far_copies(h):
            c.start()
        return carry

    lax.fori_loop(0, heads, forward, 0)

    def compute(h, carry):
        for c in far_copies(h):
            c.wait_recv()
        key, value = keys[h, 0], keys[h, 1]
        query, grad = queries[h, 0], queries[h, 1]
        far = pair_terms(query[2 * rows :], grad[2 * rows :], key[:rows], value[:rows], weight_far[...])
        near = pair_terms(
            query[rows : 2 * rows], grad[rows : 2 * rows], key[: 2 * rows], value[: 2 * rows], weight_near[...]
        )
        far_out[h, 0, 0] = far[0].astype(jnp.bfloat16)
        far_out[h, 0, 1] = far[1].astype(jnp.bfloat16)
        far_out[h, 1, 0] = (far[2] + near[2][:rows]).astype(jnp.bfloat16)
        far_out[h, 1, 1] = (far[3] + near[3][:rows]).astype(jnp.bfloat16)
        for c in far_returns(h):
            c.start()
        own = pair_terms(query[:rows], grad[:rows], key[rows:], value[rows:], weight_own[...])
        near_sum[h, 0, 0] = near[0]
        near_sum[h, 0, 1] = near[1]
        near_sum[h, 1, 0] = near[2][rows:] + own[2][:rows]
        near_sum[h, 1, 1] = near[3][rows:] + own[3][:rows]
        own_sum[h, 0, 0] = own[0]
        own_sum[h, 0, 1] = own[1]
        own_sum[h, 1, 0] = own[2][rows:]
        own_sum[h, 1, 1] = own[3][rows:]
        return carry

    lax.fori_loop(0, heads, compute, 0)

    def relay(h, carry):
        for c in far_returns(h):
            c.wait_recv()
        near_out[h] = (near_sum[h] + far_in[h].astype(jnp.float32)).astype(jnp.bfloat16)
        for c in near_returns(h):
            c.start()
        return carry

    lax.fori_loop(0, heads, relay, 0)

    def finish(h, carry):
        for c in near_returns(h):
            c.wait_recv()
        lanes = pl.ds(pl.multiple_of(h * HDIM, HDIM), HDIM)
        for side in range(2):
            for k in range(2):
                total = (own_sum[h, side, k] + near_in[h, side, k].astype(jnp.float32)).astype(jnp.bfloat16)
                out_ref[2 * side + k, :, lanes] = dot_nn(unplace, total).astype(jnp.bfloat16)
        for c in near_copies(h) + far_copies(h) + far_returns(h) + near_returns(h):
            c.wait_send()
        return carry

    lax.fori_loop(0, heads, finish, 0)


def attend(loaded, slots, lengths):
    _, rows, width = loaded.shape
    heads = width // HDIM
    blocks = lambda *lead: pltpu.VMEM((heads,) + lead + (HDIM,), jnp.bfloat16)
    totals = pltpu.VMEM((heads, 2, 2, rows, HDIM), jnp.float32)
    return pl.pallas_call(
        functools.partial(attend_kernel, "seq"),
        out_shape=jax.ShapeDtypeStruct(loaded.shape, jnp.bfloat16),
        in_specs=[
            pl.BlockSpec(memory_space=pltpu.SMEM),
            pl.BlockSpec(memory_space=pltpu.VMEM),
            pl.BlockSpec(memory_space=pltpu.VMEM),
        ],
        out_specs=pl.BlockSpec(memory_space=pltpu.VMEM),
        scratch_shapes=[
            blocks(2, 3 * rows),
            blocks(2, 3 * rows),
            blocks(2, 2, rows),
            blocks(2, 2, rows),
            blocks(2, 2, rows),
            blocks(2, 2, rows),
            totals,
            totals,
            pltpu.VMEM((rows, 2 * rows), jnp.float32),
            pltpu.VMEM((rows, 2 * rows), jnp.float32),
            pltpu.VMEM((rows, rows), jnp.float32),
            pltpu.SemaphoreType.DMA((2, 4, heads)),
            pltpu.SemaphoreType.DMA((2, 4, heads)),
        ],
        compiler_params=pltpu.CompilerParams(
            collective_id=0, has_side_effects=True, vmem_limit_bytes=48 * 1024 * 1024
        ),
        name="attend",
    )(lengths, slots, loaded)


def shards(queries, keys, values, grad_out, dest, lengths):
    row_count = queries.shape[1]
    width = queries.shape[2]
    peer_count = lax.axis_size("dp")
    per_peer = row_count // peer_count
    targets = dest[0]
    send_order = jnp.argsort(targets)
    slot_out = (targets[send_order] % row_count).reshape(1, peer_count, per_peer)
    packet = jnp.stack([queries[0], keys[0], values[0], grad_out[0]])[:, send_order].reshape(
        4, peer_count, per_peer, width
    )
    packet_in, slot_in = (
        lax.all_to_all(packet, "dp", split_axis=1, concat_axis=1, tiled=True),
        lax.all_to_all(slot_out, "dp", split_axis=1, concat_axis=1, tiled=True),
    )
    slots = jnp.broadcast_to(slot_in.reshape(1, row_count), (8, row_count))
    outgoing = attend(packet_in.reshape(4, row_count, width), slots, lengths).reshape(
        4, peer_count, per_peer, width
    )
    returned = lax.all_to_all(outgoing, "dp", split_axis=1, concat_axis=1, tiled=True).reshape(
        4, row_count, width
    )
    restored = returned[:, jnp.argsort(send_order)]
    return (restored[0][None], restored[1][None], restored[2][None], restored[3][None])


def solution(mesh):
    rows = P("seq", "dp", None)
    return jax.shard_map(
        shards,
        mesh=mesh,
        in_specs=(rows, rows, rows, rows, P("seq", "dp"), P("dp", None)),
        out_specs=(rows, rows, rows, rows),
        check_vma=False,
    )
```

time: 502 us -> 219 us (0.44)
  the two profiles are of different devices: /device:TPU:324 before, /device:TPU:1 now
where the time goes in v1:
time: 219 us
  Pallas kernels  79.1 us (36%)
  waiting for transfers between devices  73.4 us (34%)
  starting transfers between devices  33.1 us (15%)
  local copies, waits for them, and re-layouts  20.2 us (9%)
  other arithmetic  12.1 us (6%)
    pallas_call x1, Pallas kernels, attend(): pl.pallas_call(functools.partial(attend_kernel, 'seq'), out_shape=jax.Sha...  79.1 us
    all_to_all x1, waiting for transfers between devices, shards(): lax.all_to_all(packet, 'dp', split_axis=1, concat_axis=1, tiled=True)  37.6 us
    all_to_all x1, waiting for transfers between devices, shards(): lax.all_to_all(outgoing, 'dp', split_axis=1, concat_axis=1, tiled=True)  35.8 us
    all_to_all x1, starting transfers between devices, shards(): lax.all_to_all(slot_out, 'dp', split_axis=1, concat_axis=1, tiled=True)  14.5 us
    all_to_all x1, starting transfers between devices, shards(): lax.all_to_all(packet, 'dp', split_axis=1, concat_axis=1, tiled=True)  10.4 us
    all_to_all x1, starting transfers between devices, shards(): lax.all_to_all(outgoing, 'dp', split_axis=1, concat_axis=1, tiled=True)  8.17 us
    unnamed x16, local copies, waits for them, and re-layouts  7.15 us
  transfers between devices with their start and end apart: 3, of which 2 were waited for; matrix products, arithmetic and copies ran while one was open for 7% of the time, Pallas kernels for 0%

profile of v1, /device:TPU:1, one launch (start us, length us, event | category | flops | bytes accessed | tf_op | source)
XLA Modules:
  0.0 218.8 jit_solution(12622391899841415542)
XLA Ops:
  0.7 3.9 %sort.31 = (s32[192]{0:T(256)}, s32[192]{0:T(256)S(1)}) sort(s32[192]{0:T(256)} %bitcast.10, s32[192]{0:T(256)S(1)} %iota.7), dimensions={0}, to_apply=%region_0.0 | sort | flops 1536 | bytes 3072 | tf_op jit(solution)/shard_map/jit(argsort)/sort | solution.py:252
  4.6 2.0 gather_fusion
  6.8 0.6 add_select_fusion
  7.4 14.5 %all-to-all-start = ((s32[1,64,3]{2,0,1:T(1,128)}), s32[1,64,3]{2,0,1:T(1,128)S(1)}, u32[]{:S(2)}, u32[]{:S(2)}) async-start(s32[1,64,3]{2,0,1:T(1,128)} %bitcast.1), calls=%async_computation | async-start | bytes 65536 | tf_op jit(solution)/shard_map/all_to_all | solution.py:259
  21.9 1.7 copy.21
  23.6 0.6 copy.22
  24.2 0.6 copy.23
  24.9 0.6 copy.24
  25.5 3.7 %pad_maximum_fusion = bf16[4,192,1024]{2,0,1:T(4,128)(2,1)S(1)} fusion(bf16[1,192,1024]{2,0,1:T(2,128)(2,1)S(1)} %copy.24, bf16[1,192,1024]{2,0,1:T(2,128)(2,1)S(1)} %copy.23, bf16[1,192,1024]{2,0,1:T(2,128)(2,1)S(1)} %copy.22, bf16[1,192,1024]{2,0,1:T(2,128)(2,1)S(1)} %copy.21), kind=kLoop, calls=%fused_computation.3 | loop fusion | flops 6291456 | bytes 3145728 | tf_op jit(solution)/shard_map/stack | solution.py:254
  29.2 3.2 %gather_fusion.1 = bf16[192,4,1024]{2,1,0:T(4,128)(2,1)} fusion(bf16[4,192,1024]{2,0,1:T(4,128)(2,1)S(1)} %pad_maximum_fusion, s32[1024]{0:T(1024)S(1)} %pad_clamp_fusion.1), kind=kCustom, calls=%fused_computation.1 | custom fusion | bytes 3146496 | tf_op jit(solution)/shard_map/gather | solution.py:254
  32.3 10.4 %all-to-all-start.1 = ((bf16[4,64,3,1024]{3,0,2,1:T(4,128)(2,1)}), bf16[4,64,3,1024]{3,0,2,1:T(4,128)(2,1)S(1)}, u32[]{:S(2)}, u32[]{:S(2)}) async-start(bf16[4,64,3,1024]{3,0,2,1:T(4,128)(2,1)} %bitcast.3), calls=%async_computation.1 | async-start | bytes 3145728 | tf_op jit(solution)/shard_map/all_to_all | solution.py:258
  43.3 0.7 reduce.3
  44.2 37.6 %all-to-all-done.1 = bf16[4,64,3,1024]{3,0,2,1:T(4,128)(2,1)S(1)} async-done(((bf16[4,64,3,1024]{3,0,2,1:T(4,128)(2,1)}), bf16[4,64,3,1024]{3,0,2,1:T(4,128)(2,1)S(1)}, u32[]{:S(2)}, u32[]{:S(2)}) %all-to-all-start.1) | async-done | bytes 1572896 | tf_op jit(solution)/shard_map/all_to_all | solution.py:258
  82.4 79.1 %attend.1 = bf16[4,192,1024]{2,1,0:T(8,128)(2,1)S(1)} custom-call(s32[1,4]{1,0:T(1,128)S(1)} %copy-done, s32[8,192]{1,0:T(8,128)S(1)} %broadcast_in_dim.16.slots_ref, bf16[4,192,1024]{2,1,0:T(8,128)(2,1)S(1)} %copy.25.loaded_ref), custom_call_target="tpu_custom_call" | custom-call | tf_op jit(solution)/shard_map/attend/pallas_call | solution.py:215
  161.6 2.4 %copy.26 = bf16[4,192,1024]{2,0,1:T(4,128)(2,1)} copy(bf16[4,192,1024]{2,1,0:T(8,128)(2,1)S(1)} %attend.1) | data formatting | bytes 3145728 | tf_op jit(solution)/shard_map/attend/pallas_call | solution.py:215
  163.9 8.2 %all-to-all-start.2 = ((bf16[4,64,3,1024]{3,0,2,1:T(4,128)(2,1)}), bf16[4,64,3,1024]{3,0,2,1:T(4,128)(2,1)S(1)}, u32[]{:S(2)}, u32[]{:S(2)}) async-start(bf16[4,64,3,1024]{3,0,2,1:T(4,128)(2,1)} %bitcast.5), calls=%async_computation.2 | async-start | bytes 3145728 | tf_op jit(solution)/shard_map/all_to_all | solution.py:265
  172.1 3.2 %sort.32 = (s32[192]{0:T(256)}, s32[192]{0:T(256)S(1)}) sort(s32[192]{0:T(256)S(1)} %get-tuple-element.6, s32[192]{0:T(256)S(1)} %iota.8), dimensions={0}, to_apply=%region_1.2 | sort | flops 1536 | bytes 3072 | tf_op jit(solution)/shard_map/jit(argsort)/sort | solution.py:268
  175.3 35.8 %all-to-all-done.2 = bf16[4,64,3,1024]{3,0,2,1:T(4,128)(2,1)S(1)} async-done(((bf16[4,64,3,1024]{3,0,2,1:T(4,128)(2,1)}), bf16[4,64,3,1024]{3,0,2,1:T(4,128)(2,1)S(1)}, u32[]{:S(2)}, u32[]{:S(2)}) %all-to-all-start.2) | async-done | bytes 1572896 | tf_op jit(solution)/shard_map/all_to_all | solution.py:265
  211.1 1.9 gather_fusion.2
  213.0 2.3 %fusion = (bf16[1,192,1024]{2,0,1:T(2,128)(2,1)S(1)}, bf16[1,192,1024]{2,0,1:T(2,128)(2,1)S(1)}, bf16[1,192,1024]{2,0,1:T(2,128)(2,1)S(1)}, bf16[1,192,1024]{2,0,1:T(2,128)(2,1)S(1)}) fusion(bf16[4,192,1024]{2,0,1:T(4,128)(2,1)S(1)} %bitcast.12), kind=kLoop, calls=%fused_computation.10 | loop fusion | bytes 3145728 | tf_op jit(solution)/shard_map/slice | solution.py:269
  215.4 0.9 copy.27
  216.2 0.9 copy.28
  217.1 0.9 copy.29
  218.0 0.9 copy.30
  (21 shorter events, 1.5 us)
Async XLA Ops:
  0.6 23.0 %copy-start.1 = (bf16[1,192,1024]{2,1,0:T(8,128)(2,1)S(1)}, bf16[1,192,1024]{2,1,0:T(8,128)(2,1)}, u32[]{:S(2)}) copy-start(bf16[1,192,1024]{2,1,0:T(8,128)(2,1)} %param.7) | copy-start | bytes 1179652
  4.6 19.7 %copy-start.2 = (bf16[1,192,1024]{2,1,0:T(8,128)(2,1)S(1)}, bf16[1,192,1024]{2,1,0:T(8,128)(2,1)}, u32[]{:S(2)}) copy-start(bf16[1,192,1024]{2,1,0:T(8,128)(2,1)} %param.8) | copy-start | bytes 1179652
  7.4 25.0 %all-to-all-start = ((s32[1,64,3]{2,0,1:T(1,128)}), s32[1,64,3]{2,0,1:T(1,128)S(1)}, u32[]{:S(2)}, u32[]{:S(2)}) async-start(s32[1,64,3]{2,0,1:T(1,128)} %bitcast.1), calls=%async_computation | async-start | bytes 65536 | tf_op jit(solution)/shard_map/all_to_all | solution.py:259
  21.9 2.9 %copy-start.3 = (bf16[1,192,1024]{2,1,0:T(8,128)(2,1)S(1)}, bf16[1,192,1024]{2,1,0:T(8,128)(2,1)}, u32[]{:S(2)}) copy-start(bf16[1,192,1024]{2,1,0:T(8,128)(2,1)} %param.9) | copy-start | bytes 1179652
  32.3 49.4 %all-to-all-start.1 = ((bf16[4,64,3,1024]{3,0,2,1:T(4,128)(2,1)}), bf16[4,64,3,1024]{3,0,2,1:T(4,128)(2,1)S(1)}, u32[]{:S(2)}, u32[]{:S(2)}) async-start(bf16[4,64,3,1024]{3,0,2,1:T(4,128)(2,1)} %bitcast.3), calls=%async_computation.1 | async-start | bytes 3145728 | tf_op jit(solution)/shard_map/all_to_all | solution.py:258
  81.8 0.7 copy-start
  163.9 47.2 %all-to-all-start.2 = ((bf16[4,64,3,1024]{3,0,2,1:T(4,128)(2,1)}), bf16[4,64,3,1024]{3,0,2,1:T(4,128)(2,1)S(1)}, u32[]{:S(2)}, u32[]{:S(2)}) async-start(bf16[4,64,3,1024]{3,0,2,1:T(4,128)(2,1)} %bitcast.5), calls=%async_computation.2 | async-start | bytes 3145728 | tf_op jit(solution)/shard_map/all_to_all | solution.py:265

commit v2 on v1

--- a/solution.py
+++ b/solution.py
@@ -51,12 +51,24 @@
     return outputs, grad_query, grad_key, grad_value
 
 
-def attend_kernel(
-    axis,
+def whole_kernel(
     lengths_ref,
-    slots_ref,
-    loaded_ref,
+    dest_ref,
+    query_ref,
+    key_ref,
+    value_ref,
+    grad_ref,
     out_ref,
+    grad_query_ref,
+    grad_key_ref,
+    grad_value_ref,
+    mixed,
+    packed,
+    arrived,
+    packed_back,
+    arrived_back,
+    slots_out,
+    slots_in,
     keys,
     queries,
     far_out,
@@ -70,18 +82,33 @@
     weight_far,
     in_sems,
     out_sems,
+    all_sems,
 ):
     heads = keys.shape[0]
-    rows = loaded_ref.shape[1]
-    count = lax.axis_size(axis)
-    block = lax.axis_index(axis)
-    right = {axis: lax.rem(block + 1, count)}
-    left = {axis: lax.rem(block + count - 1, count)}
+    half_heads = heads // 2
+    chunks = 4 * half_heads
+    rows = query_ref.shape[0]
+    peers = lax.axis_size("dp")
+    per_peer = rows // peers
+    part = per_peer * chunks
+    me = lax.axis_index("dp")
+    count = lax.axis_size("seq")
+    block = lax.axis_index("seq")
+    right = {"seq": lax.rem(block + 1, count)}
+    left = {"seq": lax.rem(block + count - 1, count)}
+
+    def peer_at(i):
+        return lax.rem(me + lax.rem(i * 37, peers), peers)
 
     barrier = pltpu.get_barrier_semaphore()
     for neighbour in (left, right):
         pl.semaphore_signal(barrier, inc=1, device_id=neighbour, device_id_type=MESH)
-    pl.semaphore_wait(barrier, 2)
+
+    def greet(i, carry):
+        pl.semaphore_signal(barrier, inc=1, device_id={"dp": peer_at(i)}, device_id_type=MESH)
+        return carry
+
+    lax.fori_loop(1, peers, greet, 0)
 
     def copy(src, dst, sems, which, h, target):
         return pltpu.make_async_remote_copy(
@@ -117,23 +144,64 @@
             copy(near_out.at[h, 1], near_in.at[h, 1], out_sems, 3, h, left),
         )
 
-    slots = slots_ref[0:1, :]
-    place = jnp.where(
-        lax.broadcasted_iota(jnp.int32, (rows, rows), 0) == slots, jnp.float32(1.0), jnp.float32(0.0)
-    )
-    unplace = place.T.astype(jnp.bfloat16)
-    place = place.astype(jnp.bfloat16)
-    for pair in range(heads // 2):
-        lanes = pl.ds(pair * 2 * HDIM, 2 * HDIM)
-        for a, (buffer, k, start) in enumerate(
-            ((queries, 0, 0), (keys, 0, 2 * rows), (keys, 1, 2 * rows), (queries, 1, 0))
-        ):
-            placed = dot_nn(place, loaded_ref[a, :, lanes]).astype(jnp.bfloat16)
-            buffer[2 * pair, k, pl.ds(start, rows), :] = placed[:, :HDIM]
-            buffer[2 * pair + 1, k, pl.ds(start, rows), :] = placed[:, HDIM:]
-        for h in (2 * pair, 2 * pair + 1):
-            for c in near_copies(h):
-                c.start()
+    def send_half(source, target, half, which):
+        def send(i, carry):
+            peer = peer_at(i)
+            source[half, peer] = mixed[pl.ds(pl.multiple_of(peer * part, 16), part), :].astype(jnp.bfloat16)
+            copy(source.at[half, peer], target.at[half, me], all_sems, which, half, {"dp": peer}).start()
+            return carry
+
+        lax.fori_loop(1, peers, send, 0)
+        target[half, me] = mixed[pl.ds(pl.multiple_of(me * part, 16), part), :].astype(jnp.bfloat16)
+
+    def wait_all(ref, side, which, half):
+        whole = ref.at[half, pl.ds(0, peers - 1)]
+        pltpu.make_async_copy(whole, whole, all_sems.at[side, which, half]).wait()
+
+    def spread(source, half):
+        mixed[...] = source[half].reshape(peers * part, HDIM).astype(jnp.float32)
+
+    targets = dest_ref[...].astype(jnp.float32)
+    across = jnp.broadcast_to(targets, (rows, rows))
+    ranks = jnp.sum(jnp.where(across.T < across, jnp.float32(1.0), jnp.float32(0.0)), axis=0, keepdims=True)
+    steps = lax.broadcasted_iota(jnp.int32, (rows, rows), 0).astype(jnp.float32)
+    order = jnp.where(steps == ranks, jnp.float32(1.0), jnp.float32(0.0))
+    restore = order.T.astype(jnp.bfloat16)
+    order = order.astype(jnp.bfloat16)
+
+    def pack_half(half):
+        for a, ref in enumerate((query_ref, key_ref, value_ref, grad_ref)):
+            for pair in range(half_heads // 2):
+                lanes = pl.ds((half * half_heads + 2 * pair) * HDIM, 2 * HDIM)
+                sorted_rows = dot_nn(order, ref[:, lanes])
+                mixed[pl.ds(8 * pair + a, rows, stride=chunks), :] = sorted_rows[:, :HDIM]
+                mixed[pl.ds(8 * pair + 4 + a, rows, stride=chunks), :] = sorted_rows[:, HDIM:]
+
+    pack_half(0)
+    pl.semaphore_wait(barrier, peers + 1)
+    send_half(packed, arrived, 0, 0)
+
+    width = slots_out.shape[2]
+    lane = lax.broadcasted_iota(jnp.int32, (peers, 1, width), 2)
+    slots = jnp.zeros((peers, 1, width), jnp.float32)
+    first_rank = (lax.broadcasted_iota(jnp.int32, (peers, 1, rows), 0) * per_peer).astype(jnp.float32)
+    base = (lax.broadcasted_iota(jnp.int32, (peers, 1, 1), 0) * rows).astype(jnp.float32)
+    for t in range(per_peer):
+        hit = ranks.reshape(1, 1, rows) == first_rank + t
+        slot = jnp.sum(jnp.where(hit, targets.reshape(1, 1, rows), jnp.float32(0.0)), axis=2, keepdims=True) - base
+        slots = jnp.where(lane == me * per_peer + t, slot, slots)
+    slots_out[...] = slots
+
+    def send_slots(i, carry):
+        peer = peer_at(i)
+        copy(slots_out.at[peer], slots_in.at[me], all_sems, 2, 0, {"dp": peer}).start()
+        return carry
+
+    lax.fori_loop(1, peers, send_slots, 0)
+    slots_in[me] = slots_out[me]
+
+    pack_half(1)
+    send_half(packed, arrived, 1, 0)
 
     weight = jnp.float32(1.0 / (REACH * rows))
     first = block * rows
@@ -145,16 +213,40 @@
         mask = pair_weight(lengths_ref, query_first, ref.shape[0], key_first, ref.shape[1])
         ref[...] = jnp.where(mask, weight, jnp.float32(0.0))
 
-    def forward(h, carry):
+    everyone = slots_in.at[pl.ds(0, peers - 1)]
+    pltpu.make_async_copy(everyone, everyone, all_sems.at[1, 2, 0]).wait()
+    slot_row = jnp.sum(slots_in[...], axis=0)[:, :rows]
+    place = jnp.where(steps == slot_row, jnp.float32(1.0), jnp.float32(0.0))
+    unplace = place.T.astype(jnp.bfloat16)
+    place = place.astype(jnp.bfloat16)
+
+    def place_half(half):
+        wait_all(arrived, 1, 0, half)
+        spread(arrived, half)
+        for i in range(half_heads):
+            h = half * half_heads + i
+            for a, (buffer, k, start) in enumerate(
+                ((queries, 0, 0), (keys, 0, 2 * rows), (keys, 1, 2 * rows), (queries, 1, 0))
+            ):
+                came = mixed[pl.ds(4 * i + a, rows, stride=chunks), :].astype(jnp.bfloat16)
+                buffer[h, k, pl.ds(start, rows), :] = dot_nn(place, came).astype(jnp.bfloat16)
+            for c in near_copies(h):
+                c.start()
+
+    def each_head(half, step):
+        def run(h, carry):
+            step(h)
+            return carry
+
+        lax.fori_loop(half * half_heads, (half + 1) * half_heads, run, 0)
+
+    def forward(h):
         for c in near_copies(h):
             c.wait_recv()
         for c in far_copies(h):
             c.start()
-        return carry
-
-    lax.fori_loop(0, heads, forward, 0)
-
-    def compute(h, carry):
+
+    def compute(h):
         for c in far_copies(h):
             c.wait_recv()
         key, value = keys[h, 0], keys[h, 1]
@@ -178,50 +270,82 @@
         own_sum[h, 0, 1] = own[1]
         own_sum[h, 1, 0] = own[2][rows:]
         own_sum[h, 1, 1] = own[3][rows:]
-        return carry
-
-    lax.fori_loop(0, heads, compute, 0)
-
-    def relay(h, carry):
+
+    def relay(h):
         for c in far_returns(h):
             c.wait_recv()
         near_out[h] = (near_sum[h] + far_in[h].astype(jnp.float32)).astype(jnp.bfloat16)
         for c in near_returns(h):
             c.start()
-        return carry
-
-    lax.fori_loop(0, heads, relay, 0)
-
-    def finish(h, carry):
-        for c in near_returns(h):
-            c.wait_recv()
-        lanes = pl.ds(pl.multiple_of(h * HDIM, HDIM), HDIM)
-        for side in range(2):
-            for k in range(2):
-                total = (own_sum[h, side, k] + near_in[h, side, k].astype(jnp.float32)).astype(jnp.bfloat16)
-                out_ref[2 * side + k, :, lanes] = dot_nn(unplace, total).astype(jnp.bfloat16)
+
+    def finish_half(half):
+        for i in range(half_heads):
+            h = half * half_heads + i
+            for c in near_returns(h):
+                c.wait_recv()
+            for side in range(2):
+                for k in range(2):
+                    total = (own_sum[h, side, k] + near_in[h, side, k].astype(jnp.float32)).astype(jnp.bfloat16)
+                    mixed[pl.ds(4 * i + 2 * side + k, rows, stride=chunks), :] = dot_nn(unplace, total)
+        send_half(packed_back, arrived_back, half, 1)
+
+    def restore_half(half):
+        wait_all(arrived_back, 1, 1, half)
+        spread(arrived_back, half)
+        for i in range(half_heads):
+            lanes = pl.ds((half * half_heads + i) * HDIM, HDIM)
+            for a, ref in enumerate((out_ref, grad_query_ref, grad_key_ref, grad_value_ref)):
+                came = mixed[pl.ds(4 * i + a, rows, stride=chunks), :].astype(jnp.bfloat16)
+                ref[:, lanes] = dot_nn(restore, came).astype(jnp.bfloat16)
+
+    place_half(0)
+    each_head(0, forward)
+    each_head(0, compute)
+    place_half(1)
+    each_head(0, relay)
+    each_head(1, forward)
+    finish_half(0)
+    each_head(1, compute)
+    each_head(1, relay)
+    restore_half(0)
+    finish_half(1)
+
+    def settle(h):
         for c in near_copies(h) + far_copies(h) + far_returns(h) + near_returns(h):
             c.wait_send()
-        return carry
-
-    lax.fori_loop(0, heads, finish, 0)
-
-
-def attend(loaded, slots, lengths):
-    _, rows, width = loaded.shape
+
+    each_head(0, settle)
+    each_head(1, settle)
+    for half in range(2):
+        wait_all(packed, 0, 0, half)
+        wait_all(packed_back, 0, 1, half)
+    pltpu.make_async_copy(everyone, everyone, all_sems.at[0, 2, 0]).wait()
+    restore_half(1)
+
+
+def shards(queries, keys, values, grad_out, dest, lengths):
+    _, rows, width = queries.shape
     heads = width // HDIM
+    peers = lax.axis_size("dp")
+    part = rows // peers * 2 * heads
     blocks = lambda *lead: pltpu.VMEM((heads,) + lead + (HDIM,), jnp.bfloat16)
     totals = pltpu.VMEM((heads, 2, 2, rows, HDIM), jnp.float32)
-    return pl.pallas_call(
-        functools.partial(attend_kernel, "seq"),
-        out_shape=jax.ShapeDtypeStruct(loaded.shape, jnp.bfloat16),
-        in_specs=[
-            pl.BlockSpec(memory_space=pltpu.SMEM),
-            pl.BlockSpec(memory_space=pltpu.VMEM),
-            pl.BlockSpec(memory_space=pltpu.VMEM),
-        ],
-        out_specs=pl.BlockSpec(memory_space=pltpu.VMEM),
+    halves = pltpu.VMEM((2, peers, part, HDIM), jnp.bfloat16)
+    slots = pltpu.VMEM((peers, 1, (rows + 127) // 128 * 128), jnp.float32)
+    vmem = pl.BlockSpec(memory_space=pltpu.VMEM)
+    results = pl.pallas_call(
+        whole_kernel,
+        out_shape=[jax.ShapeDtypeStruct((rows, width), jnp.bfloat16)] * 4,
+        in_specs=[pl.BlockSpec(memory_space=pltpu.SMEM)] + [vmem] * 5,
+        out_specs=[vmem] * 4,
         scratch_shapes=[
+            pltpu.VMEM((peers * part, HDIM), jnp.float32),
+            halves,
+            halves,
+            halves,
+            halves,
+            slots,
+            slots,
             blocks(2, 3 * rows),
             blocks(2, 3 * rows),
             blocks(2, 2, rows),
@@ -235,38 +359,14 @@
             pltpu.VMEM((rows, rows), jnp.float32),
             pltpu.SemaphoreType.DMA((2, 4, heads)),
             pltpu.SemaphoreType.DMA((2, 4, heads)),
+            pltpu.SemaphoreType.DMA((2, 3, 2)),
         ],
         compiler_params=pltpu.CompilerParams(
-            collective_id=0, has_side_effects=True, vmem_limit_bytes=48 * 1024 * 1024
+            collective_id=0, has_side_effects=True, vmem_limit_bytes=52 * 1024 * 1024
         ),
-        name="attend",
-    )(lengths, slots, loaded)
-
-
-def shards(queries, keys, values, grad_out, dest, lengths):
-    row_count = queries.shape[1]
-    width = queries.shape[2]
-    peer_count = lax.axis_size("dp")
-    per_peer = row_count // peer_count
-    targets = dest[0]
-    send_order = jnp.argsort(targets)
-    slot_out = (targets[send_order] % row_count).reshape(1, peer_count, per_peer)
-    packet = jnp.stack([queries[0], keys[0], values[0], grad_out[0]])[:, send_order].reshape(
-        4, peer_count, per_peer, width
-    )
-    packet_in, slot_in = (
-        lax.all_to_all(packet, "dp", split_axis=1, concat_axis=1, tiled=True),
-        lax.all_to_all(slot_out, "dp", split_axis=1, concat_axis=1, tiled=True),
-    )
-    slots = jnp.broadcast_to(slot_in.reshape(1, row_count), (8, row_count))
-    outgoing = attend(packet_in.reshape(4, row_count, width), slots, lengths).reshape(
-        4, peer_count, per_peer, width
-    )
-    returned = lax.all_to_all(outgoing, "dp", split_axis=1, concat_axis=1, tiled=True).reshape(
-        4, row_count, width
-    )
-    restored = returned[:, jnp.argsort(send_order)]
-    return (restored[0][None], restored[1][None], restored[2][None], restored[3][None])
+        name="whole",
+    )(lengths, dest, queries[0], keys[0], values[0], grad_out[0])
+    return tuple(result[None] for result in results)
 
 
 def solution(mesh):

time: 219 us -> 145 us (0.66)
  waiting for transfers between devices: 73.4 us -> 0 us
  Pallas kernels: 79.1 us -> 140 us
  starting transfers between devices: 33.1 us -> 0 us
  local copies, waits for them, and re-layouts: 20.2 us -> 4.65 us
  other arithmetic: 12.1 us -> 0 us
    all_to_all x3 -> x0, waiting for transfers between devices: 73.4 us -> none  [the longest x1 37.6 us: shards(): lax.all_to_all(packet, 'dp', split_axis=1, concat_axis=1, tiled=True)]
    pallas_call x1, Pallas kernels: 79.1 us -> 140 us  [shards(): pl.pallas_call(whole_kernel, out_shape=[jax.ShapeDtypeStruct((rows, width...]
    all_to_all x3 -> x0, starting transfers between devices: 33.1 us -> none  [the longest x1 14.5 us: shards(): lax.all_to_all(slot_out, 'dp', split_axis=1, concat_axis=1, tiled=True)]
    gather x3 -> x0, local copies, waits for them, and re-layouts: 7.11 us -> none  [the longest x1 3.16 us: shards(): jnp.stack([queries[0], keys[0], values[0], grad_out[0]])[:, send_order]]
    sort x2 -> x0, other arithmetic: 7.06 us -> none  [the longest x1 3.89 us: shards(): send_order = jnp.argsort(targets)]
    another operation x1 -> x0, other arithmetic: 3.7 us -> none  [shards(): jnp.stack([queries[0], keys[0], values[0], grad_out[0]])[:, send_order]]
    unnamed x16 -> x10, local copies, waits for them, and re-layouts: 7.15 us -> 4.65 us
    pallas_call x1 -> x0, local copies, waits for them, and re-layouts: 2.37 us -> none  [attend(): pl.pallas_call(functools.partial(attend_kernel, 'seq'), out_shape=jax.Sha...]
  transfers between devices with their start and end apart: 3 -> 0, of which waited for: 2 -> 0; matrix products, arithmetic and copies ran while one was open for 7% -> 0% of each run, Pallas kernels for 0% -> 0%
where the time goes in v2:
time: 145 us
  Pallas kernels  140 us (97%)
  local copies, waits for them, and re-layouts  4.65 us (3%)
    pallas_call x1, Pallas kernels, shards(): pl.pallas_call(whole_kernel, out_shape=[jax.ShapeDtypeStruct((rows, width...  140 us
    unnamed x10, local copies, waits for them, and re-layouts  4.65 us

profile of v2, /device:TPU:1, one launch (start us, length us, event | category | flops | bytes accessed | tf_op | source)
XLA Modules:
  0.0 144.8 jit_solution(13362874158960016963)
XLA Ops:
  0.6 0.0 copy-start.1
  0.6 0.0 copy-start.2
  0.7 0.7 copy-done.1
  1.3 0.0 copy-done.2
  1.3 0.0 copy-start
  1.3 1.0 copy-done
  2.3 139.5 %whole.1 = (bf16[192,1024]{1,0:T(8,128)(2,1)S(1)}, bf16[192,1024]{1,0:T(8,128)(2,1)S(1)}, bf16[192,1024]{1,0:T(8,128)(2,1)S(1)}, bf16[192,1024]{1,0:T(8,128)(2,1)S(1)}) custom-call(s32[1,4]{1,0:T(1,128)S(1)} %copy-done.2, s32[1,192]{1,0:T(1,128)S(1)} %copy-done.1, bf16[192,1024]{1,0:T(8,128)(2,1)S(1)} %bitcast.12, bf16[192,1024]{1,0:T(8,128)(2,1)} %bitcast.13, ...), custom_call_target="tpu_custom_call" | custom-call | tf_op jit(solution)/shard_map/whole/pallas_call | solution.py:336
  141.8 0.7 copy.14
  142.6 0.7 copy.15
  143.3 0.7 copy.16
  144.1 0.7 copy.17
Async XLA Ops:
  0.6 0.7 copy-start.1
  0.6 0.7 copy-start.2
  1.3 1.0 copy-start

commit v3 on v2

--- a/solution.py
+++ b/solution.py
@@ -9,6 +9,7 @@
 
 HDIM = 128
 REACH = 4
+GROUPS = 4
 MESH = pl.DeviceIdType.MESH
 
 
@@ -67,6 +68,10 @@
     arrived,
     packed_back,
     arrived_back,
+    handed,
+    came,
+    handed_back,
+    came_back,
     slots_out,
     slots_in,
     keys,
@@ -85,27 +90,29 @@
     all_sems,
 ):
     heads = keys.shape[0]
-    half_heads = heads // 2
-    chunks = 4 * half_heads
+    group_heads = heads // GROUPS
+    chunks = 4 * group_heads
     rows = query_ref.shape[0]
     peers = lax.axis_size("dp")
+    chips = peers // 2
     per_peer = rows // peers
-    part = per_peer * chunks
+    part = 2 * per_peer * chunks
+    shared = per_peer * chips
     me = lax.axis_index("dp")
+    chip = me // 2
+    core = lax.rem(me, 2)
+    sibling = {"dp": 2 * chip + 1 - core}
     count = lax.axis_size("seq")
     block = lax.axis_index("seq")
     right = {"seq": lax.rem(block + 1, count)}
     left = {"seq": lax.rem(block + count - 1, count)}
 
-    def peer_at(i):
-        return lax.rem(me + lax.rem(i * 37, peers), peers)
-
     barrier = pltpu.get_barrier_semaphore()
     for neighbour in (left, right):
         pl.semaphore_signal(barrier, inc=1, device_id=neighbour, device_id_type=MESH)
 
     def greet(i, carry):
-        pl.semaphore_signal(barrier, inc=1, device_id={"dp": peer_at(i)}, device_id_type=MESH)
+        pl.semaphore_signal(barrier, inc=1, device_id={"dp": lax.rem(me + i, peers)}, device_id_type=MESH)
         return carry
 
     lax.fori_loop(1, peers, greet, 0)
@@ -144,64 +151,79 @@
             copy(near_out.at[h, 1], near_in.at[h, 1], out_sems, 3, h, left),
         )
 
-    def send_half(source, target, half, which):
+    def send_group(source, target, g, which):
         def send(i, carry):
-            peer = peer_at(i)
-            source[half, peer] = mixed[pl.ds(pl.multiple_of(peer * part, 16), part), :].astype(jnp.bfloat16)
-            copy(source.at[half, peer], target.at[half, me], all_sems, which, half, {"dp": peer}).start()
+            other = lax.rem(chip + i, chips)
+            source[g, other] = mixed[pl.ds(pl.multiple_of(other * part, 16), part), :].astype(jnp.bfloat16)
+            copy(source.at[g, other], target.at[g, chip], all_sems, which, g, {"dp": 2 * other + core}).start()
             return carry
 
-        lax.fori_loop(1, peers, send, 0)
-        target[half, me] = mixed[pl.ds(pl.multiple_of(me * part, 16), part), :].astype(jnp.bfloat16)
-
-    def wait_all(ref, side, which, half):
-        whole = ref.at[half, pl.ds(0, peers - 1)]
-        pltpu.make_async_copy(whole, whole, all_sems.at[side, which, half]).wait()
-
-    def spread(source, half):
-        mixed[...] = source[half].reshape(peers * part, HDIM).astype(jnp.float32)
+        lax.fori_loop(1, chips, send, 0)
+        target[g, chip] = mixed[pl.ds(pl.multiple_of(chip * part, 16), part), :].astype(jnp.bfloat16)
+
+    def wait_all(ref, side, which, g):
+        whole = ref.at[g, pl.ds(0, chips - 1)]
+        pltpu.make_async_copy(whole, whole, all_sems.at[side, which, g]).wait()
+
+    def hand_copy(source, target, g, which):
+        return copy(source.at[g], target.at[g, :, pl.ds(shared, shared)], all_sems, which, g, sibling)
+
+    def hand_over(source, given, target, g, which):
+        wait_all(source, 1, which, g)
+        mixed[...] = source[g].reshape(chips * part, HDIM).astype(jnp.float32)
+        for c in range(chunks):
+            for t in range(per_peer):
+                first = mixed[pl.ds(t * chunks + c, chips, stride=part), :]
+                second = mixed[pl.ds((per_peer + t) * chunks + c, chips, stride=part), :]
+                target[g, c, pl.ds(t * chips, chips), :] = jnp.where(core == 0, first, second).astype(jnp.bfloat16)
+                given[g, c, pl.ds(t * chips, chips), :] = jnp.where(core == 0, second, first).astype(jnp.bfloat16)
+        hand_copy(given, target, g, which + 3).start()
 
     targets = dest_ref[...].astype(jnp.float32)
     across = jnp.broadcast_to(targets, (rows, rows))
     ranks = jnp.sum(jnp.where(across.T < across, jnp.float32(1.0), jnp.float32(0.0)), axis=0, keepdims=True)
     steps = lax.broadcasted_iota(jnp.int32, (rows, rows), 0).astype(jnp.float32)
-    order = jnp.where(steps == ranks, jnp.float32(1.0), jnp.float32(0.0))
-    restore = order.T.astype(jnp.bfloat16)
-    order = order.astype(jnp.bfloat16)
-
-    def pack_half(half):
+    order = jnp.where(steps == ranks, jnp.float32(1.0), jnp.float32(0.0)).astype(jnp.bfloat16)
+    holder = jnp.floor((ranks + 0.5) * (1.0 / per_peer))
+    holder_chip = jnp.floor((holder + 0.5) * 0.5)
+    away = jnp.abs(holder - 2.0 * holder_chip - core.astype(jnp.float32))
+    spots = away * shared + (ranks - holder * per_peer) * chips + holder_chip
+    restore = jnp.where(steps == spots, jnp.float32(1.0), jnp.float32(0.0)).T.astype(jnp.bfloat16)
+
+    def pack_group(g):
         for a, ref in enumerate((query_ref, key_ref, value_ref, grad_ref)):
-            for pair in range(half_heads // 2):
-                lanes = pl.ds((half * half_heads + 2 * pair) * HDIM, 2 * HDIM)
-                sorted_rows = dot_nn(order, ref[:, lanes])
-                mixed[pl.ds(8 * pair + a, rows, stride=chunks), :] = sorted_rows[:, :HDIM]
-                mixed[pl.ds(8 * pair + 4 + a, rows, stride=chunks), :] = sorted_rows[:, HDIM:]
-
-    pack_half(0)
+            sorted_rows = dot_nn(order, ref[:, pl.ds(g * group_heads * HDIM, group_heads * HDIM)])
+            for i in range(group_heads):
+                mixed[pl.ds(4 * i + a, rows, stride=chunks), :] = sorted_rows[:, i * HDIM : (i + 1) * HDIM]
+        send_group(packed, arrived, g, 0)
+
     pl.semaphore_wait(barrier, peers + 1)
-    send_half(packed, arrived, 0, 0)
+    pack_group(0)
 
     width = slots_out.shape[2]
     lane = lax.broadcasted_iota(jnp.int32, (peers, 1, width), 2)
+    receiver = lax.broadcasted_iota(jnp.int32, (peers, 1, 1), 0)
+    apart = jnp.where(lax.rem(receiver, 2) == core, 0, shared)
     slots = jnp.zeros((peers, 1, width), jnp.float32)
-    first_rank = (lax.broadcasted_iota(jnp.int32, (peers, 1, rows), 0) * per_peer).astype(jnp.float32)
-    base = (lax.broadcasted_iota(jnp.int32, (peers, 1, 1), 0) * rows).astype(jnp.float32)
+    base = (receiver * rows).astype(jnp.float32)
+    first_rank = (receiver * per_peer).astype(jnp.float32)
     for t in range(per_peer):
         hit = ranks.reshape(1, 1, rows) == first_rank + t
         slot = jnp.sum(jnp.where(hit, targets.reshape(1, 1, rows), jnp.float32(0.0)), axis=2, keepdims=True) - base
-        slots = jnp.where(lane == me * per_peer + t, slot, slots)
+        slots = jnp.where(lane == apart + t * chips + chip, slot, slots)
+        slots = jnp.where(lane == width // 2 + me * per_peer + t, slot, slots)
     slots_out[...] = slots
 
     def send_slots(i, carry):
-        peer = peer_at(i)
+        peer = lax.rem(me + i, peers)
         copy(slots_out.at[peer], slots_in.at[me], all_sems, 2, 0, {"dp": peer}).start()
         return carry
 
     lax.fori_loop(1, peers, send_slots, 0)
     slots_in[me] = slots_out[me]
 
-    pack_half(1)
-    send_half(packed, arrived, 1, 0)
+    for g in range(1, GROUPS):
+        pack_group(g)
 
     weight = jnp.float32(1.0 / (REACH * rows))
     first = block * rows
@@ -215,30 +237,31 @@
 
     everyone = slots_in.at[pl.ds(0, peers - 1)]
     pltpu.make_async_copy(everyone, everyone, all_sems.at[1, 2, 0]).wait()
-    slot_row = jnp.sum(slots_in[...], axis=0)[:, :rows]
-    place = jnp.where(steps == slot_row, jnp.float32(1.0), jnp.float32(0.0))
-    unplace = place.T.astype(jnp.bfloat16)
-    place = place.astype(jnp.bfloat16)
-
-    def place_half(half):
-        wait_all(arrived, 1, 0, half)
-        spread(arrived, half)
-        for i in range(half_heads):
-            h = half * half_heads + i
+    slot_row = jnp.sum(slots_in[...], axis=0)
+    place = jnp.where(steps == slot_row[:, :rows], jnp.float32(1.0), jnp.float32(0.0)).astype(jnp.bfloat16)
+    back = slot_row[:, width // 2 : width // 2 + rows]
+    unplace = jnp.where(steps == back, jnp.float32(1.0), jnp.float32(0.0)).T.astype(jnp.bfloat16)
+
+    def each_head(g, step):
+        def run(h, carry):
+            step(h)
+            return carry
+
+        lax.fori_loop(g * group_heads, (g + 1) * group_heads, run, 0)
+
+    def unpack(g):
+        hand_over(arrived, handed, came, g, 0)
+
+    def place_group(g):
+        hand_copy(handed, came, g, 3).wait_recv()
+        for i in range(group_heads):
+            h = g * group_heads + i
             for a, (buffer, k, start) in enumerate(
                 ((queries, 0, 0), (keys, 0, 2 * rows), (keys, 1, 2 * rows), (queries, 1, 0))
             ):
-                came = mixed[pl.ds(4 * i + a, rows, stride=chunks), :].astype(jnp.bfloat16)
-                buffer[h, k, pl.ds(start, rows), :] = dot_nn(place, came).astype(jnp.bfloat16)
+                buffer[h, k, pl.ds(start, rows), :] = dot_nn(place, came[g, 4 * i + a]).astype(jnp.bfloat16)
             for c in near_copies(h):
                 c.start()
-
-    def each_head(half, step):
-        def run(h, carry):
-            step(h)
-            return carry
-
-        lax.fori_loop(half * half_heads, (half + 1) * half_heads, run, 0)
 
     def forward(h):
         for c in near_copies(h):
@@ -278,60 +301,76 @@
         for c in near_returns(h):
             c.start()
 
-    def finish_half(half):
-        for i in range(half_heads):
-            h = half * half_heads + i
+    def finish(g):
+        for i in range(group_heads):
+            h = g * group_heads + i
             for c in near_returns(h):
                 c.wait_recv()
             for side in range(2):
                 for k in range(2):
                     total = (own_sum[h, side, k] + near_in[h, side, k].astype(jnp.float32)).astype(jnp.bfloat16)
                     mixed[pl.ds(4 * i + 2 * side + k, rows, stride=chunks), :] = dot_nn(unplace, total)
-        send_half(packed_back, arrived_back, half, 1)
-
-    def restore_half(half):
-        wait_all(arrived_back, 1, 1, half)
-        spread(arrived_back, half)
-        for i in range(half_heads):
-            lanes = pl.ds((half * half_heads + i) * HDIM, HDIM)
+        send_group(packed_back, arrived_back, g, 1)
+
+    def unpack_back(g):
+        hand_over(arrived_back, handed_back, came_back, g, 1)
+
+    def restore_group(g):
+        hand_copy(handed_back, came_back, g, 4).wait_recv()
+        for i in range(group_heads):
+            lanes = pl.ds((g * group_heads + i) * HDIM, HDIM)
             for a, ref in enumerate((out_ref, grad_query_ref, grad_key_ref, grad_value_ref)):
-                came = mixed[pl.ds(4 * i + a, rows, stride=chunks), :].astype(jnp.bfloat16)
-                ref[:, lanes] = dot_nn(restore, came).astype(jnp.bfloat16)
-
-    place_half(0)
+                ref[:, lanes] = dot_nn(restore, came_back[g, 4 * i + a]).astype(jnp.bfloat16)
+
+    unpack(0)
+    place_group(0)
     each_head(0, forward)
-    each_head(0, compute)
-    place_half(1)
-    each_head(0, relay)
-    each_head(1, forward)
-    finish_half(0)
-    each_head(1, compute)
-    each_head(1, relay)
-    restore_half(0)
-    finish_half(1)
+    for g in range(1, GROUPS):
+        unpack(g)
+        place_group(g)
+        each_head(g - 1, compute)
+        if g > 1:
+            finish(g - 2)
+        each_head(g, forward)
+        each_head(g - 1, relay)
+    each_head(GROUPS - 1, compute)
+    finish(GROUPS - 2)
+    each_head(GROUPS - 1, relay)
+    for g in range(GROUPS - 2):
+        unpack_back(g)
+        restore_group(g)
+    finish(GROUPS - 1)
+    unpack_back(GROUPS - 2)
+    restore_group(GROUPS - 2)
 
     def settle(h):
         for c in near_copies(h) + far_copies(h) + far_returns(h) + near_returns(h):
             c.wait_send()
 
-    each_head(0, settle)
-    each_head(1, settle)
-    for half in range(2):
-        wait_all(packed, 0, 0, half)
-        wait_all(packed_back, 0, 1, half)
+    for g in range(GROUPS):
+        each_head(g, settle)
+        wait_all(packed, 0, 0, g)
+        hand_copy(handed, came, g, 3).wait_send()
     pltpu.make_async_copy(everyone, everyone, all_sems.at[0, 2, 0]).wait()
-    restore_half(1)
+    unpack_back(GROUPS - 1)
+    restore_group(GROUPS - 1)
+    for g in range(GROUPS):
+        wait_all(packed_back, 0, 1, g)
+        hand_copy(handed_back, came_back, g, 4).wait_send()
 
 
 def shards(queries, keys, values, grad_out, dest, lengths):
     _, rows, width = queries.shape
     heads = width // HDIM
     peers = lax.axis_size("dp")
-    part = rows // peers * 2 * heads
+    chunks = 4 * heads // GROUPS
+    part = rows // peers * 2 * chunks
     blocks = lambda *lead: pltpu.VMEM((heads,) + lead + (HDIM,), jnp.bfloat16)
     totals = pltpu.VMEM((heads, 2, 2, rows, HDIM), jnp.float32)
-    halves = pltpu.VMEM((2, peers, part, HDIM), jnp.bfloat16)
-    slots = pltpu.VMEM((peers, 1, (rows + 127) // 128 * 128), jnp.float32)
+    pieces = pltpu.VMEM((GROUPS, peers // 2, part, HDIM), jnp.bfloat16)
+    handed = pltpu.VMEM((GROUPS, chunks, rows // 2, HDIM), jnp.bfloat16)
+    came = pltpu.VMEM((GROUPS, chunks, rows, HDIM), jnp.bfloat16)
+    slots = pltpu.VMEM((peers, 1, (rows + 127) // 128 * 256), jnp.float32)
     vmem = pl.BlockSpec(memory_space=pltpu.VMEM)
     results = pl.pallas_call(
         whole_kernel,
@@ -339,11 +378,15 @@
         in_specs=[pl.BlockSpec(memory_space=pltpu.SMEM)] + [vmem] * 5,
         out_specs=[vmem] * 4,
         scratch_shapes=[
-            pltpu.VMEM((peers * part, HDIM), jnp.float32),
-            halves,
-            halves,
-            halves,
-            halves,
+            pltpu.VMEM((peers // 2 * part, HDIM), jnp.float32),
+            pieces,
+            pieces,
+            pieces,
+            pieces,
+            handed,
+            came,
+            handed,
+            came,
             slots,
             slots,
             blocks(2, 3 * rows),
@@ -359,7 +402,7 @@
             pltpu.VMEM((rows, rows), jnp.float32),
             pltpu.SemaphoreType.DMA((2, 4, heads)),
             pltpu.SemaphoreType.DMA((2, 4, heads)),
-            pltpu.SemaphoreType.DMA((2, 3, 2)),
+            pltpu.SemaphoreType.DMA((2, 5, GROUPS)),
         ],
         compiler_params=pltpu.CompilerParams(
             collective_id=0, has_side_effects=True, vmem_limit_bytes=52 * 1024 * 1024

time: 145 us -> 135 us (0.931)
  Pallas kernels: 140 us -> 129 us
    pallas_call x1, Pallas kernels: 140 us -> 129 us  [shards(): pl.pallas_call(whole_kernel, out_shape=[jax.ShapeDtypeStruct((rows, width...]
where the time goes in v3:
time: 135 us
  Pallas kernels  129 us (96%)
  local copies, waits for them, and re-layouts  4.65 us (3%)
    pallas_call x1, Pallas kernels, shards(): pl.pallas_call(whole_kernel, out_shape=[jax.ShapeDtypeStruct((rows, width...  129 us
    unnamed x10, local copies, waits for them, and re-layouts  4.65 us

profile of v3, /device:TPU:1, one launch (start us, length us, event | category | flops | bytes accessed | tf_op | source)
XLA Modules:
  0.0 134.8 jit_solution(15902459890858585677)
XLA Ops:
  0.6 0.0 copy-start.1
  0.6 0.0 copy-start.2
  0.7 0.7 copy-done.1
  1.3 0.0 copy-done.2
  1.3 0.0 copy-start
  1.3 1.0 copy-done
  2.3 129.5 %whole.1 = (bf16[192,1024]{1,0:T(8,128)(2,1)S(1)}, bf16[192,1024]{1,0:T(8,128)(2,1)S(1)}, bf16[192,1024]{1,0:T(8,128)(2,1)S(1)}, bf16[192,1024]{1,0:T(8,128)(2,1)S(1)}) custom-call(s32[1,4]{1,0:T(1,128)S(1)} %copy-done.2, s32[1,192]{1,0:T(1,128)S(1)} %copy-done.1, bf16[192,1024]{1,0:T(8,128)(2,1)S(1)} %bitcast.12, bf16[192,1024]{1,0:T(8,128)(2,1)} %bitcast.13, ...), custom_call_target="tpu_custom_call" | custom-call | tf_op jit(solution)/shard_map/whole/pallas_call | solution.py:375
  131.8 0.7 copy.14
  132.5 0.7 copy.15
  133.3 0.7 copy.16
  134.0 0.7 copy.17
Async XLA Ops:
  0.6 0.7 copy-start.1
  0.6 0.7 copy-start.2
  1.3 1.0 copy-start

commit v4 on v3

--- a/solution.py
+++ b/solution.py
@@ -63,6 +63,7 @@
     grad_query_ref,
     grad_key_ref,
     grad_value_ref,
+    loaded,
     mixed,
     packed,
     arrived,
@@ -88,6 +89,7 @@
     in_sems,
     out_sems,
     all_sems,
+    load_sems,
 ):
     heads = keys.shape[0]
     group_heads = heads // GROUPS
@@ -107,6 +109,13 @@
     right = {"seq": lax.rem(block + 1, count)}
     left = {"seq": lax.rem(block + count - 1, count)}
 
+    loads = [
+        pltpu.make_async_copy(ref, loaded.at[a], load_sems.at[a])
+        for a, ref in enumerate((query_ref, key_ref, value_ref, grad_ref))
+    ]
+    for c in loads:
+        c.start()
+
     barrier = pltpu.get_barrier_semaphore()
     for neighbour in (left, right):
         pl.semaphore_signal(barrier, inc=1, device_id=neighbour, device_id_type=MESH)
@@ -175,9 +184,13 @@
             for t in range(per_peer):
                 first = mixed[pl.ds(t * chunks + c, chips, stride=part), :]
                 second = mixed[pl.ds((per_peer + t) * chunks + c, chips, stride=part), :]
-                target[g, c, pl.ds(t * chips, chips), :] = jnp.where(core == 0, first, second).astype(jnp.bfloat16)
                 given[g, c, pl.ds(t * chips, chips), :] = jnp.where(core == 0, second, first).astype(jnp.bfloat16)
         hand_copy(given, target, g, which + 3).start()
+        for c in range(chunks):
+            for t in range(per_peer):
+                first = mixed[pl.ds(t * chunks + c, chips, stride=part), :]
+                second = mixed[pl.ds((per_peer + t) * chunks + c, chips, stride=part), :]
+                target[g, c, pl.ds(t * chips, chips), :] = jnp.where(core == 0, first, second).astype(jnp.bfloat16)
 
     targets = dest_ref[...].astype(jnp.float32)
     across = jnp.broadcast_to(targets, (rows, rows))
@@ -191,14 +204,13 @@
     restore = jnp.where(steps == spots, jnp.float32(1.0), jnp.float32(0.0)).T.astype(jnp.bfloat16)
 
     def pack_group(g):
-        for a, ref in enumerate((query_ref, key_ref, value_ref, grad_ref)):
-            sorted_rows = dot_nn(order, ref[:, pl.ds(g * group_heads * HDIM, group_heads * HDIM)])
+        for a in range(4):
+            sorted_rows = dot_nn(order, loaded[a, :, pl.ds(g * group_heads * HDIM, group_heads * HDIM)])
             for i in range(group_heads):
                 mixed[pl.ds(4 * i + a, rows, stride=chunks), :] = sorted_rows[:, i * HDIM : (i + 1) * HDIM]
+        if g == 0:
+            pl.semaphore_wait(barrier, peers + 1)
         send_group(packed, arrived, g, 0)
-
-    pl.semaphore_wait(barrier, peers + 1)
-    pack_group(0)
 
     width = slots_out.shape[2]
     lane = lax.broadcasted_iota(jnp.int32, (peers, 1, width), 2)
@@ -214,6 +226,9 @@
         slots = jnp.where(lane == width // 2 + me * per_peer + t, slot, slots)
     slots_out[...] = slots
 
+    for c in loads:
+        c.wait()
+    pack_group(0)
     def send_slots(i, carry):
         peer = lax.rem(me + i, peers)
         copy(slots_out.at[peer], slots_in.at[me], all_sems, 2, 0, {"dp": peer}).start()
@@ -359,6 +374,15 @@
         hand_copy(handed_back, came_back, g, 4).wait_send()
 
 
+def deliver_kernel(*refs):
+    sems = refs[-1]
+    moves = [pltpu.make_async_copy(refs[a], refs[4 + a], sems.at[a]) for a in range(4)]
+    for move in moves:
+        move.start()
+    for move in moves:
+        move.wait()
+
+
 def shards(queries, keys, values, grad_out, dest, lengths):
     _, rows, width = queries.shape
     heads = width // HDIM
@@ -375,9 +399,10 @@
     results = pl.pallas_call(
         whole_kernel,
         out_shape=[jax.ShapeDtypeStruct((rows, width), jnp.bfloat16)] * 4,
-        in_specs=[pl.BlockSpec(memory_space=pltpu.SMEM)] + [vmem] * 5,
+        in_specs=[pl.BlockSpec(memory_space=pltpu.SMEM), vmem] + [pl.BlockSpec(memory_space=pltpu.HBM)] * 4,
         out_specs=[vmem] * 4,
         scratch_shapes=[
+            pltpu.VMEM((4, rows, width), jnp.bfloat16),
             pltpu.VMEM((peers // 2 * part, HDIM), jnp.float32),
             pieces,
             pieces,
@@ -403,12 +428,22 @@
             pltpu.SemaphoreType.DMA((2, 4, heads)),
             pltpu.SemaphoreType.DMA((2, 4, heads)),
             pltpu.SemaphoreType.DMA((2, 5, GROUPS)),
+            pltpu.SemaphoreType.DMA((4,)),
         ],
         compiler_params=pltpu.CompilerParams(
             collective_id=0, has_side_effects=True, vmem_limit_bytes=52 * 1024 * 1024
         ),
         name="whole",
     )(lengths, dest, queries[0], keys[0], values[0], grad_out[0])
+    anywhere = [pl.BlockSpec(memory_space=pl.ANY)] * 4
+    results = pl.pallas_call(
+        deliver_kernel,
+        out_shape=[jax.ShapeDtypeStruct((rows, width), jnp.bfloat16)] * 4,
+        in_specs=anywhere,
+        out_specs=anywhere,
+        scratch_shapes=[pltpu.SemaphoreType.DMA((4,))],
+        name="deliver",
+    )(*results)
     return tuple(result[None] for result in results)
 
 

time: 135 us -> 183 us (1.36)
  Pallas kernels: 129 us -> 177 us
    pallas_call x0 -> x1, Pallas kernels: none -> 48.8 us  [shards(): pl.pallas_call(deliver_kernel, out_shape=[jax.ShapeDtypeStruct((rows, wid...]
    unnamed x10 -> x14, local copies, waits for them, and re-layouts: 4.65 us -> 4.67 us
where the time goes in v4:
time: 183 us
  Pallas kernels  177 us (97%)
  local copies, waits for them, and re-layouts  4.67 us (3%)
    pallas_call x1, Pallas kernels, shards(): pl.pallas_call(whole_kernel, out_shape=[jax.ShapeDtypeStruct((rows, width...  129 us
    pallas_call x1, Pallas kernels, shards(): pl.pallas_call(deliver_kernel, out_shape=[jax.ShapeDtypeStruct((rows, wid...  48.8 us
    unnamed x14, local copies, waits for them, and re-layouts  4.67 us

profile of v4, /device:TPU:1, one launch (start us, length us, event | category | flops | bytes accessed | tf_op | source)
XLA Modules:
  0.0 182.9 jit_solution(1852370016783117717)
XLA Ops:
  0.6 0.0 copy-start.5
  0.6 0.0 copy-start.6
  0.7 0.7 copy-done.5
  1.3 0.0 copy-done.6
  1.3 0.0 copy-start
  1.3 1.0 copy-done
  2.3 128.7 %whole.1 = (bf16[192,1024]{1,0:T(8,128)(2,1)S(1)}, bf16[192,1024]{1,0:T(8,128)(2,1)S(1)}, bf16[192,1024]{1,0:T(8,128)(2,1)S(1)}, bf16[192,1024]{1,0:T(8,128)(2,1)S(1)}) custom-call(s32[1,4]{1,0:T(1,128)S(1)} %copy-done.6, s32[1,192]{1,0:T(1,128)S(1)} %copy-done.5, bf16[192,1024]{1,0:T(8,128)(2,1)S(1)} %bitcast.8, bf16[192,1024]{1,0:T(8,128)(2,1)} %bitcast.9, ...), custom_call_target="tpu_custom_call" | custom-call | tf_op jit(solution)/shard_map/whole/pallas_call | solution.py:399
  131.0 0.0 copy-start.1
  131.0 0.7 copy-done.1
  131.7 0.0 copy-start.2
  131.7 0.8 copy-done.2
  132.5 0.0 copy-start.3
  132.5 0.8 copy-done.3
  133.2 0.0 copy-start.4
  133.2 0.8 copy-done.4
  134.0 48.8 %deliver.1 = (bf16[192,1024]{1,0:T(8,128)(2,1)}, bf16[192,1024]{1,0:T(8,128)(2,1)}, bf16[192,1024]{1,0:T(8,128)(2,1)}, bf16[192,1024]{1,0:T(8,128)(2,1)}) custom-call(bf16[192,1024]{1,0:T(8,128)(2,1)} %copy-done.1, bf16[192,1024]{1,0:T(8,128)(2,1)} %copy-done.2, bf16[192,1024]{1,0:T(8,128)(2,1)} %copy-done.3, bf16[192,1024]{1,0:T(8,128)(2,1)} %copy-done.4), custom_call_target="tpu_custom_call" | custom-call | tf_op jit(solution)/shard_map/deliver/pallas_call | solution.py:439
Async XLA Ops:
  0.6 0.7 copy-start.5
  0.6 0.7 copy-start.6
  1.3 1.0 copy-start
  131.0 0.7 copy-start.1
  131.7 0.8 copy-start.2
  132.5 0.8 copy-start.3
  133.2 0.8 copy-start.4

commit v5 on v4

--- a/solution.py
+++ b/solution.py
@@ -9,7 +9,8 @@
 
 HDIM = 128
 REACH = 4
-GROUPS = 4
+SIZES = (1, 2, 2, 2, 1)
+GROUPS = len(SIZES)
 MESH = pl.DeviceIdType.MESH
 
 
@@ -92,14 +93,13 @@
     load_sems,
 ):
     heads = keys.shape[0]
-    group_heads = heads // GROUPS
-    chunks = 4 * group_heads
     rows = query_ref.shape[0]
     peers = lax.axis_size("dp")
     chips = peers // 2
     per_peer = rows // peers
-    part = 2 * per_peer * chunks
     shared = per_peer * chips
+    firsts = [sum(SIZES[:g]) for g in range(GROUPS)]
+    parts = [(2 * per_peer * 4 * size + 15) // 16 * 16 for size in SIZES]
     me = lax.axis_index("dp")
     chip = me // 2
     core = lax.rem(me, 2)
@@ -161,25 +161,31 @@
         )
 
     def send_group(source, target, g, which):
+        part = parts[g]
+
         def send(i, carry):
             other = lax.rem(chip + i, chips)
-            source[g, other] = mixed[pl.ds(pl.multiple_of(other * part, 16), part), :].astype(jnp.bfloat16)
-            copy(source.at[g, other], target.at[g, chip], all_sems, which, g, {"dp": 2 * other + core}).start()
+            source[g, other, pl.ds(0, part), :] = mixed[pl.ds(pl.multiple_of(other * part, 16), part), :].astype(jnp.bfloat16)
+            piece, place_there = source.at[g, other, pl.ds(0, part)], target.at[g, chip, pl.ds(0, part)]
+            copy(piece, place_there, all_sems, which, g, {"dp": 2 * other + core}).start()
             return carry
 
         lax.fori_loop(1, chips, send, 0)
-        target[g, chip] = mixed[pl.ds(pl.multiple_of(chip * part, 16), part), :].astype(jnp.bfloat16)
+        target[g, chip, pl.ds(0, part), :] = mixed[pl.ds(pl.multiple_of(chip * part, 16), part), :].astype(jnp.bfloat16)
 
     def wait_all(ref, side, which, g):
-        whole = ref.at[g, pl.ds(0, chips - 1)]
+        whole = ref.at[g, pl.ds(0, chips - 1), pl.ds(0, parts[g])]
         pltpu.make_async_copy(whole, whole, all_sems.at[side, which, g]).wait()
 
     def hand_copy(source, target, g, which):
-        return copy(source.at[g], target.at[g, :, pl.ds(shared, shared)], all_sems, which, g, sibling)
+        used = pl.ds(0, 4 * SIZES[g])
+        return copy(source.at[g, used], target.at[g, used, pl.ds(shared, shared)], all_sems, which, g, sibling)
 
     def hand_over(source, given, target, g, which):
         wait_all(source, 1, which, g)
-        mixed[...] = source[g].reshape(chips * part, HDIM).astype(jnp.float32)
+        part, chunks = parts[g], 4 * SIZES[g]
+        came_rows = source[g, :, pl.ds(0, part), :].reshape(chips * part, HDIM)
+        mixed[pl.ds(0, chips * part), :] = came_rows.astype(jnp.float32)
         for c in range(chunks):
             for t in range(per_peer):
                 first = mixed[pl.ds(t * chunks + c, chips, stride=part), :]
@@ -196,18 +202,25 @@
     across = jnp.broadcast_to(targets, (rows, rows))
     ranks = jnp.sum(jnp.where(across.T < across, jnp.float32(1.0), jnp.float32(0.0)), axis=0, keepdims=True)
     steps = lax.broadcasted_iota(jnp.int32, (rows, rows), 0).astype(jnp.float32)
-    order = jnp.where(steps == ranks, jnp.float32(1.0), jnp.float32(0.0)).astype(jnp.bfloat16)
     holder = jnp.floor((ranks + 0.5) * (1.0 / per_peer))
     holder_chip = jnp.floor((holder + 0.5) * 0.5)
+    mailed = (ranks - holder_chip * (2 * per_peer)) * chips + holder_chip
+    order = jnp.where(steps == mailed, jnp.float32(1.0), jnp.float32(0.0)).astype(jnp.bfloat16)
     away = jnp.abs(holder - 2.0 * holder_chip - core.astype(jnp.float32))
     spots = away * shared + (ranks - holder * per_peer) * chips + holder_chip
     restore = jnp.where(steps == spots, jnp.float32(1.0), jnp.float32(0.0)).T.astype(jnp.bfloat16)
 
+    mixed[...] = jnp.zeros_like(mixed)
+
+    def mix(g, c, values):
+        for u in range(2 * per_peer):
+            mixed[pl.ds(u * 4 * SIZES[g] + c, chips, stride=parts[g]), :] = values[u * chips : (u + 1) * chips]
+
     def pack_group(g):
         for a in range(4):
-            sorted_rows = dot_nn(order, loaded[a, :, pl.ds(g * group_heads * HDIM, group_heads * HDIM)])
-            for i in range(group_heads):
-                mixed[pl.ds(4 * i + a, rows, stride=chunks), :] = sorted_rows[:, i * HDIM : (i + 1) * HDIM]
+            sorted_rows = dot_nn(order, loaded[a, :, pl.ds(firsts[g] * HDIM, SIZES[g] * HDIM)])
+            for i in range(SIZES[g]):
+                mix(g, 4 * i + a, sorted_rows[:, i * HDIM : (i + 1) * HDIM])
         if g == 0:
             pl.semaphore_wait(barrier, peers + 1)
         send_group(packed, arrived, g, 0)
@@ -223,7 +236,7 @@
         hit = ranks.reshape(1, 1, rows) == first_rank + t
         slot = jnp.sum(jnp.where(hit, targets.reshape(1, 1, rows), jnp.float32(0.0)), axis=2, keepdims=True) - base
         slots = jnp.where(lane == apart + t * chips + chip, slot, slots)
-        slots = jnp.where(lane == width // 2 + me * per_peer + t, slot, slots)
+        slots = jnp.where(lane == width // 2 + (core * per_peer + t) * chips + chip, slot, slots)
     slots_out[...] = slots
 
     for c in loads:
@@ -262,15 +275,15 @@
             step(h)
             return carry
 
-        lax.fori_loop(g * group_heads, (g + 1) * group_heads, run, 0)
+        lax.fori_loop(firsts[g], firsts[g] + SIZES[g], run, 0)
 
     def unpack(g):
         hand_over(arrived, handed, came, g, 0)
 
     def place_group(g):
         hand_copy(handed, came, g, 3).wait_recv()
-        for i in range(group_heads):
-            h = g * group_heads + i
+        for i in range(SIZES[g]):
+            h = firsts[g] + i
             for a, (buffer, k, start) in enumerate(
                 ((queries, 0, 0), (keys, 0, 2 * rows), (keys, 1, 2 * rows), (queries, 1, 0))
             ):
@@ -317,14 +330,14 @@
             c.start()
 
     def finish(g):
-        for i in range(group_heads):
-            h = g * group_heads + i
+        for i in range(SIZES[g]):
+            h = firsts[g] + i
             for c in near_returns(h):
                 c.wait_recv()
             for side in range(2):
                 for k in range(2):
                     total = (own_sum[h, side, k] + near_in[h, side, k].astype(jnp.float32)).astype(jnp.bfloat16)
-                    mixed[pl.ds(4 * i + 2 * side + k, rows, stride=chunks), :] = dot_nn(unplace, total)
+                    mix(g, 4 * i + 2 * side + k, dot_nn(unplace, total))
         send_group(packed_back, arrived_back, g, 1)
 
     def unpack_back(g):
@@ -332,8 +345,8 @@
 
     def restore_group(g):
         hand_copy(handed_back, came_back, g, 4).wait_recv()
-        for i in range(group_heads):
-            lanes = pl.ds((g * group_heads + i) * HDIM, HDIM)
+        for i in range(SIZES[g]):
+            lanes = pl.ds((firsts[g] + i) * HDIM, HDIM)
             for a, ref in enumerate((out_ref, grad_query_ref, grad_key_ref, grad_value_ref)):
                 ref[:, lanes] = dot_nn(restore, came_back[g, 4 * i + a]).astype(jnp.bfloat16)
 
@@ -348,15 +361,16 @@
             finish(g - 2)
         each_head(g, forward)
         each_head(g - 1, relay)
+        if g > 2:
+            unpack_back(g - 3)
+            restore_group(g - 3)
     each_head(GROUPS - 1, compute)
     finish(GROUPS - 2)
     each_head(GROUPS - 1, relay)
-    for g in range(GROUPS - 2):
+    finish(GROUPS - 1)
+    for g in range(GROUPS - 3, GROUPS - 1):
         unpack_back(g)
         restore_group(g)
-    finish(GROUPS - 1)
-    unpack_back(GROUPS - 2)
-    restore_group(GROUPS - 2)
 
     def settle(h):
         for c in near_copies(h) + far_copies(h) + far_returns(h) + near_returns(h):
@@ -374,20 +388,11 @@
         hand_copy(handed_back, came_back, g, 4).wait_send()
 
 
-def deliver_kernel(*refs):
-    sems = refs[-1]
-    moves = [pltpu.make_async_copy(refs[a], refs[4 + a], sems.at[a]) for a in range(4)]
-    for move in moves:
-        move.start()
-    for move in moves:
-        move.wait()
-
-
 def shards(queries, keys, values, grad_out, dest, lengths):
     _, rows, width = queries.shape
     heads = width // HDIM
     peers = lax.axis_size("dp")
-    chunks = 4 * heads // GROUPS
+    chunks = 4 * max(SIZES)
     part = rows // peers * 2 * chunks
     blocks = lambda *lead: pltpu.VMEM((heads,) + lead + (HDIM,), jnp.bfloat16)
     totals = pltpu.VMEM((heads, 2, 2, rows, HDIM), jnp.float32)
@@ -435,15 +440,6 @@
         ),
         name="whole",
     )(lengths, dest, queries[0], keys[0], values[0], grad_out[0])
-    anywhere = [pl.BlockSpec(memory_space=pl.ANY)] * 4
-    results = pl.pallas_call(
-        deliver_kernel,
-        out_shape=[jax.ShapeDtypeStruct((rows, width), jnp.bfloat16)] * 4,
-        in_specs=anywhere,
-        out_specs=anywhere,
-        scratch_shapes=[pltpu.SemaphoreType.DMA((4,))],
-        name="deliver",
-    )(*results)
     return tuple(result[None] for result in results)
 
 

time: 183 us -> 134 us (0.73)
  Pallas kernels: 177 us -> 128 us
    pallas_call x1 -> x0, Pallas kernels: 48.8 us -> none  [shards(): pl.pallas_call(deliver_kernel, out_shape=[jax.ShapeDtypeStruct((rows, wid...]
    unnamed x14 -> x10, local copies, waits for them, and re-layouts: 4.67 us -> 4.65 us
where the time goes in v5:
time: 134 us
  Pallas kernels  128 us (96%)
  local copies, waits for them, and re-layouts  4.65 us (3%)
    pallas_call x1, Pallas kernels, shards(): pl.pallas_call(whole_kernel, out_shape=[jax.ShapeDtypeStruct((rows, width...  128 us
    unnamed x10, local copies, waits for them, and re-layouts  4.65 us

profile of v5, /device:TPU:1, one launch (start us, length us, event | category | flops | bytes accessed | tf_op | source)
XLA Modules:
  0.0 133.7 jit_solution(6795491220311015759)
XLA Ops:
  0.6 0.0 copy-start.1
  0.6 0.0 copy-start.2
  0.7 0.7 copy-done.1
  1.3 0.0 copy-done.2
  1.3 0.0 copy-start
  1.3 1.0 copy-done
  2.3 128.4 %whole.1 = (bf16[192,1024]{1,0:T(8,128)(2,1)S(1)}, bf16[192,1024]{1,0:T(8,128)(2,1)S(1)}, bf16[192,1024]{1,0:T(8,128)(2,1)S(1)}, bf16[192,1024]{1,0:T(8,128)(2,1)S(1)}) custom-call(s32[1,4]{1,0:T(1,128)S(1)} %copy-done.2, s32[1,192]{1,0:T(1,128)S(1)} %copy-done.1, bf16[192,1024]{1,0:T(8,128)(2,1)S(1)} %bitcast.12, bf16[192,1024]{1,0:T(8,128)(2,1)} %bitcast.13, ...), custom_call_target="tpu_custom_call" | custom-call | tf_op jit(solution)/shard_map/whole/pallas_call | solution.py:404
  130.7 0.7 copy.14
  131.5 0.7 copy.15
  132.2 0.7 copy.16
  133.0 0.7 copy.17
Async XLA Ops:
  0.6 0.7 copy-start.1
  0.6 0.7 copy-start.2
  1.3 1.0 copy-start

commit v6 on v5

--- a/solution.py
+++ b/solution.py
@@ -353,23 +353,23 @@
     unpack(0)
     place_group(0)
     each_head(0, forward)
+    unpack(1)
     for g in range(1, GROUPS):
-        unpack(g)
         place_group(g)
         each_head(g - 1, compute)
         if g > 1:
             finish(g - 2)
         each_head(g, forward)
+        if g + 1 < GROUPS:
+            unpack(g + 1)
         each_head(g - 1, relay)
-        if g > 2:
-            unpack_back(g - 3)
-            restore_group(g - 3)
     each_head(GROUPS - 1, compute)
     finish(GROUPS - 2)
     each_head(GROUPS - 1, relay)
     finish(GROUPS - 1)
-    for g in range(GROUPS - 3, GROUPS - 1):
+    for g in range(GROUPS - 1):
         unpack_back(g)
+    for g in range(GROUPS - 1):
         restore_group(g)
 
     def settle(h):

time: 134 us -> 134 us (level)
  no operation moved by 1% of the time
where the time goes in v6:
time: 134 us
  Pallas kernels  128 us (96%)
  local copies, waits for them, and re-layouts  4.65 us (3%)
    pallas_call x1, Pallas kernels, shards(): pl.pallas_call(whole_kernel, out_shape=[jax.ShapeDtypeStruct((rows, width...  128 us
    unnamed x10, local copies, waits for them, and re-layouts  4.65 us

profile of v6, /device:TPU:1, one launch (start us, length us, event | category | flops | bytes accessed | tf_op | source)
XLA Modules:
  0.0 133.7 jit_solution(8806522137506173927)
XLA Ops:
  0.6 0.0 copy-start.1
  0.6 0.0 copy-start.2
  0.7 0.7 copy-done.1
  1.3 0.0 copy-done.2
  1.3 0.0 copy-start
  1.3 1.0 copy-done
  2.3 128.4 %whole.1 = (bf16[192,1024]{1,0:T(8,128)(2,1)S(1)}, bf16[192,1024]{1,0:T(8,128)(2,1)S(1)}, bf16[192,1024]{1,0:T(8,128)(2,1)S(1)}, bf16[192,1024]{1,0:T(8,128)(2,1)S(1)}) custom-call(s32[1,4]{1,0:T(1,128)S(1)} %copy-done.2, s32[1,192]{1,0:T(1,128)S(1)} %copy-done.1, bf16[192,1024]{1,0:T(8,128)(2,1)S(1)} %bitcast.12, bf16[192,1024]{1,0:T(8,128)(2,1)} %bitcast.13, ...), custom_call_target="tpu_custom_call" | custom-call | tf_op jit(solution)/shard_map/whole/pallas_call | solution.py:404
  130.8 0.7 copy.14
  131.5 0.7 copy.15
  132.3 0.7 copy.16
  133.0 0.7 copy.17
Async XLA Ops:
  0.6 0.7 copy-start.1
  0.6 0.7 copy-start.2
  1.3 1.0 copy-start
